TPU v7x, 32 devices: a whole 2x2x4 slice. The times are simulated.
32 devices in a mesh: tm: 8 (over z, core), height: 4 (over y, x).
Axes of the slice: x: 2, y: 2, z: 4, core: 2. Of those that a mesh axis runs over, the one named last changes fastest.
Arguments:
- block_input: bfloat16 [16, 8, 160, 384], P('tm', 'height'), may hold values from -400 to 400
- gain: float32 [384], replicated, may hold values from 0.1 to 1.9
- kernel: bfloat16 [384, 10368], P('height'), may hold values from -0.0625 to 0.0625
- cotangent: bfloat16 [16, 8, 160, 384], P('tm', 'height'), may hold values from -11 to 11
Outputs:
- input_grad: bfloat16 [16, 8, 160, 384], P('tm', 'height')
- kernel_grad: float32 [384, 27, 384], P('height', None, 'tm')
- gain_grad: float32 [384], replicated
- bias_grad: float32 [384], replicated
All inputs are finite; a program needn't handle non-finite values.
Results may differ from a plain program's by a relative error of at most 0.0029.
Values may be sent and summed in bfloat16 or wider, within the bound.
A program may use at most 128 MiB of HBM per device.

v0:
```python
import math

import jax
import jax.numpy as jnp
from jax import lax
from jax.sharding import PartitionSpec as P


def from_behind(value, axis, steps):
    count = lax.axis_size(axis)
    leading, last = (max(0, -steps), min(count, count - steps))
    return lax.ppermute(value, axis, [(source, source + steps) for source in range(leading, last)])


def padded(block, sides, width):
    for axis, dim in sides:
        count = lax.axis_size(axis)
        forward = [(i, i + 1) for i in range(count - 1)]
        backward = [(target, source) for source, target in forward]
        low = lax.ppermute(
            lax.slice_in_dim(block, block.shape[dim] - width, None, axis=dim), axis, forward
        )
        high = lax.ppermute(lax.slice_in_dim(block, 0, width, axis=dim), axis, backward)
        block = jnp.concatenate([low, block, high], axis=dim)
    return block


def tap_offsets(k):
    return (k // 9, k // 3 % 3, k % 3)


def shards(block_input, gain, kernel, cotangent):
    frames, rows, width, chans = block_input.shape
    total_cells = frames * lax.axis_size("tm") * rows * lax.axis_size("height") * width
    scale = 1.0 / math.sqrt(total_cells)
    xfull = block_input.astype(jnp.float32)
    inv_rms = lax.rsqrt(jnp.mean(xfull * xfull, axis=-1, keepdims=True) + 1e-06)
    normed = xfull * inv_rms
    pre = normed * gain
    sig = jax.nn.sigmoid(pre)
    act = (pre * sig).astype(jnp.bfloat16)
    later = from_behind(cotangent, "tm", -1)
    grad_ext = jnp.concatenate([cotangent, later], axis=0)
    grad_rim = padded(grad_ext, (("height", 1),), 1)
    grad_pad = jnp.pad(grad_rim, ((0, 0), (0, 0), (1, 1), (0, 0)))
    earlier = from_behind(act, "tm", 1)
    act_ext = jnp.concatenate([earlier, act], axis=0)
    act_rim = padded(act_ext, (("height", 1),), 1)
    act_pad = jnp.pad(act_rim, ((0, 0), (0, 0), (1, 1), (0, 0)))
    grad_flat = cotangent.reshape(-1, chans)
    outputs = []
    for k in range(27):
        tap_ktime, tap_krow, tap_kcol = tap_offsets(k)
        left = act_pad[
            tap_ktime : tap_ktime + frames, tap_krow : tap_krow + rows, tap_kcol : tap_kcol + width
        ].reshape(-1, chans)
        left, right = (left, grad_flat)
        outputs.append(
            lax.dot_general(
                left, right, (((0,), (0,)), ((), ())), preferred_element_type=jnp.float32
            )
        )
    partial_rows = lax.psum_scatter(
        jnp.stack(outputs, axis=1), "height", scatter_dimension=0, tiled=True
    )
    kernel_grad = lax.psum_scatter(partial_rows, "tm", scatter_dimension=2, tiled=True) * scale
    piece = lax.all_gather(kernel, "height", axis=0, tiled=True)
    taps = piece.reshape(piece.shape[0], 27, chans)
    total = jnp.zeros((frames * rows * width, piece.shape[0]), jnp.float32)
    for k in range(27):
        ktime, krow, kcol = tap_offsets(k)
        total = total + lax.dot_general(
            grad_pad[
                2 - ktime : 2 - ktime + frames,
                2 - krow : 2 - krow + rows,
                2 - kcol : 2 - kcol + width,
            ].reshape(-1, chans),
            taps[:, k, :],
            (((1,), (1,)), ((), ())),
            preferred_element_type=jnp.float32,
        )
    act_grad = total.reshape(frames, rows, width, piece.shape[0])
    pre_grad = act_grad * sig * (1.0 + pre * (1.0 - sig))
    gain_local = jnp.sum(pre_grad * normed, axis=(0, 1, 2))
    bias_local = jnp.sum(cotangent.astype(jnp.float32), axis=(0, 1, 2))
    gain_total, bias_total = lax.psum((gain_local, bias_local), ("tm", "height"))
    normed_grad = pre_grad * gain
    input_grad = inv_rms * (
        normed_grad - normed * jnp.mean(normed_grad * normed, axis=-1, keepdims=True)
    )
    return (input_grad.astype(jnp.bfloat16), kernel_grad, gain_total * scale, bias_total * scale)


def solution(mesh):
    return jax.shard_map(
        shards,
        mesh=mesh,
        in_specs=(
            P("tm", "height", None, None),
            P(),
            P("height", None),
            P("tm", "height", None, None),
        ),
        out_specs=(P("tm", "height", None, None), P("height", None, "tm"), P(), P()),
        check_vma=False,
    )
```

profile of v0, /device:TPU:0, one launch (start us, length us, event | category | flops | bytes accessed | tf_op | source)
XLA Modules:
  0.0 467.2 jit_solution(14188545519104434128)
XLA Ops:
  10.3 1.6 collective-permute-done
  13.4 5.5 %collective-permute-start.1 = (bf16[4,1,160,384]{3,2,1,0:T(8,128)(2,1)S(1)}, bf16[4,1,160,384]{3,2,1,0:T(8,128)(2,1)S(1)}, u32[]{:S(2)}, u32[]{:S(2)}) collective-permute-start(bf16[4,1,160,384]{3,2,1,0:T(8,128)(2,1)S(1)} %get-tuple-element.51), channel_id=1, source_target_pairs={{0,1},{1,2},{2,3},{4,5},{5,6},{6,7},{8,9},{9,10},{10,11},{12,13},{... | collective-permute-start | bytes 1474568 | tf_op jit(solution)/shard_map/ppermute | solution.py:20
  19.2 4.6 collective-permute-done.2
  23.8 9.6 %collective-permute-done.1 = bf16[4,1,160,384]{3,2,1,0:T(8,128)(2,1)S(1)} collective-permute-done((bf16[4,1,160,384]{3,2,1,0:T(8,128)(2,1)S(1)}, bf16[4,1,160,384]{3,2,1,0:T(8,128)(2,1)S(1)}, u32[]{:S(2)}, u32[]{:S(2)}) %collective-permute-start.1) | collective-permute-done | bytes 491552 | tf_op jit(solution)/shard_map/ppermute | solution.py:20
  33.4 1.3 fusion.56
  35.5 3.6 fusion.103
  39.1 77.1 %all-gather.2.cloned.1.call-done = bf16[384,10368]{1,0:T(8,128)(2,1)} async-done(((bf16[96,10368]{1,0:T(8,128)(2,1)}), bf16[384,10368]{1,0:T(8,128)(2,1)}) %all-gather.2.cloned.1.call-update) | async-done | bytes 7962640 | tf_op jit(solution)/shard_map/all_gather | solution.py:67
  116.2 11.3 %copy.38 = bf16[384,10368]{0,1:T(8,128)(2,1)} copy(bf16[384,10368]{1,0:T(8,128)(2,1)} %all-gather.2.cloned.1.call-done) | data formatting | bytes 15925248 | tf_op jit(solution)/shard_map/all_gather | solution.py:67
  127.5 1.7 fusion.75
  129.2 2.3 fusion.76
  131.5 1.6 fusion.77
  133.2 1.5 fusion.78
  134.6 1.6 fusion.79
  136.2 1.5 fusion.80
  144.4 1.4 fusion.95
  145.8 1.4 fusion.96
  147.2 1.4 fusion.97
  148.6 1.4 fusion.98
  150.0 1.4 fusion.100
  151.4 1.4 fusion.99
  152.9 5.6 %fusion.4 = f32[640,384]{1,0:T(8,128)} fusion(f32[640,384]{1,0:T(8,128)S(1)} %fusion.75, f32[640,384]{1,0:T(8,128)S(1)} %fusion.76, f32[640,384]{1,0:T(8,128)S(1)} %fusion.77, bf16[640,384]{1,0:T(8,128)(2,1)} %bitcast.463, f32[640,384]{1,0:T(8,128)S(1)} %fusion.78, f32[640,384]{1,0:T(8,128)S(1)} %fusion.79, f32[640,384]{1,0:T(8,128)S(1)} %fusion.80, ...), kind=kOutput, calls=%fused_computation.22 | convolution fusion | flops 195133440 | bytes 27328512 | tf_op jit(solution)/shard_map/dot_general | solution.py:72
  158.5 2.2 fusion.49
  162.0 1.8 collective-permute-start.3
  163.8 1.4 collective-permute-done.3
  166.6 4.6 collective-permute-start.4
  171.2 5.0 %collective-permute-done.5 = bf16[4,1,160,384]{3,2,1,0:T(8,128)(2,1)S(1)} collective-permute-done((bf16[4,1,160,384]{3,2,1,0:T(8,128)(2,1)S(1)}, bf16[4,1,160,384]{3,2,1,0:T(8,128)(2,1)S(1)}, u32[]{:S(2)}, u32[]{:S(2)}) %collective-permute-start.5) | collective-permute-done | bytes 491552 | tf_op jit(solution)/shard_map/ppermute | solution.py:23
  176.2 1.7 collective-permute-done.4
  179.1 1.3 fusion.31
  180.4 1.3 fusion.10
  185.6 1.3 fusion.27
  188.2 1.3 fusion.9
  189.5 1.3 fusion.25
  190.9 1.3 fusion.24
  193.5 1.3 fusion.23
  196.1 1.3 fusion.11
  197.4 1.4 fusion.21
  198.8 1.3 fusion.20
  200.1 1.3 fusion.7
  201.4 1.3 fusion.19
  205.3 1.3 fusion.17
  206.6 1.3 fusion.16
  209.3 1.3 fusion.14
  211.9 1.3 fusion.5
  213.2 1.3 fusion.12
  214.6 166.4 %reduce-scatter.3.cloned.1.call-done = f32[96,27,384]{2,0,1:T(8,128)} async-done(((f32[384,27,384]{2,0,1:T(8,128)}), f32[96,27,384]{2,0,1:T(8,128)}) %reduce-scatter.3.cloned.1.call-update) | async-done | bytes 3981328 | tf_op jit(solution)/shard_map/reduce_scatter | solution.py:63
  381.0 6.2 %copy.66 = f32[96,27,384]{0,1,2:T(8,128)} copy(f32[96,27,384]{2,0,1:T(8,128)} %reduce-scatter.3.cloned.1.call-done) | data formatting | bytes 7962624 | tf_op jit(solution)/shard_map/reduce_scatter | solution.py:63
  387.3 41.3 %all-reduce.2 = (f32[384]{0:T(512)S(1)}, f32[384]{0:T(512)S(1)}) all-reduce(f32[384]{0:T(512)S(1)} %get-tuple-element.16, f32[384]{0:T(512)S(1)} %convert_reduce_fusion), channel_id=1, replica_groups=mesh['tm'=8,'height'=4] {'tm','height'}, use_global_device_ids=true, to_apply=%region_5.6 | all-reduce | flops 768 | bytes 6144 | tf_op jit(solution)/shard_map/psum | solution.py:86
  429.1 29.0 %reduce-scatter.5.cloned.1.call-done = f32[96,27,48]{0,1,2:T(8,128)} async-done(((f32[96,27,384]{0,1,2:T(8,128)}), f32[96,27,48]{0,1,2:T(8,128)}) %reduce-scatter.5.cloned.1.call-update) | async-done | bytes 497680 | tf_op jit(solution)/shard_map/reduce_scatter | solution.py:66
  (89 shorter events, 32.0 us)
Async XLA Ops:
  7.2 11.8 %copy-start.1 = (bf16[2,2,160,384]{3,2,1,0:T(8,128)(2,1)S(1)}, bf16[2,2,160,384]{3,2,1,0:T(8,128)(2,1)}, u32[]{:S(2)}) copy-start(bf16[2,2,160,384]{3,2,1,0:T(8,128)(2,1)} %param.4) | copy-start | bytes 1474564
  7.2 109.0 %all-gather.2.cloned.1.call-start = ((), (), s32[]{:S(2)}) async-start(), calls=%async_computation.2 | async-start | bytes 9953280 | tf_op jit(solution)/shard_map/all_gather | solution.py:67
  7.9 373.1 %reduce-scatter.3.cloned.1.call-start = ((), (), s32[]{:S(2)}) async-start(), calls=%async_computation.3 | async-start | bytes 19906560 | tf_op jit(solution)/shard_map/reduce_scatter | solution.py:63
  8.0 4.0 collective-permute-start
  11.9 22.8 %copy-start.3 = (bf16[2,2,160,384]{3,2,1,0:T(8,128)(2,1)}, bf16[2,2,160,384]{3,2,1,0:T(8,128)(2,1)S(1)}, u32[]{:S(2)}) copy-start(bf16[2,2,160,384]{3,2,1,0:T(8,128)(2,1)S(1)} %collective-permute-done) | copy-start | bytes 1474564
  12.1 11.6 %collective-permute-start.2 = (bf16[4,1,160,384]{3,2,1,0:T(8,128)(2,1)S(1)}, bf16[4,1,160,384]{3,2,1,0:T(8,128)(2,1)S(1)}, u32[]{:S(2)}, u32[]{:S(2)}) collective-permute-start(bf16[4,1,160,384]{3,2,1,0:T(8,128)(2,1)S(1)} %get-tuple-element.52), channel_id=1, source_target_pairs={{1,0},{2,1},{3,2},{5,4},{6,5},{7,6},{9,8},{10,9},{11,10},{13,12},{... | collective-permute-start | bytes 1474568 | tf_op jit(solution)/shard_map/ppermute | solution.py:23
  13.4 20.0 %collective-permute-start.1 = (bf16[4,1,160,384]{3,2,1,0:T(8,128)(2,1)S(1)}, bf16[4,1,160,384]{3,2,1,0:T(8,128)(2,1)S(1)}, u32[]{:S(2)}, u32[]{:S(2)}) collective-permute-start(bf16[4,1,160,384]{3,2,1,0:T(8,128)(2,1)S(1)} %get-tuple-element.51), channel_id=1, source_target_pairs={{0,1},{1,2},{2,3},{4,5},{5,6},{6,7},{8,9},{9,10},{10,11},{12,13},{... | collective-permute-start | bytes 1474568 | tf_op jit(solution)/shard_map/ppermute | solution.py:20
  127.5 5.6 %copy-start.2 = (bf16[2,2,160,384]{3,2,1,0:T(8,128)(2,1)S(1)}, bf16[2,2,160,384]{3,2,1,0:T(8,128)(2,1)}, u32[]{:S(2)}) copy-start(bf16[2,2,160,384]{3,2,1,0:T(8,128)(2,1)} %param.7) | copy-start | bytes 1474564
  127.5 8.7 %copy-start = (bf16[384,10368]{0,1:T(8,128)(2,1)S(1)}, bf16[384,10368]{0,1:T(8,128)(2,1)}, u32[]{:S(2)}) copy-start(bf16[384,10368]{0,1:T(8,128)(2,1)} %copy.38) | copy-start | bytes 23887876
  129.2 8.5 %copy-start.11 = (bf16[2,2,160,384]{3,2,1,0:T(8,128)(2,1)S(1)}, bf16[2,2,160,384]{3,2,1,0:T(8,128)(2,1)}, u32[]{:S(2)}) copy-start(bf16[2,2,160,384]{3,2,1,0:T(8,128)(2,1)} %get-tuple-element.40) | copy-start | bytes 1474564
  131.5 6.7 %copy-start.19 = (bf16[2,2,160,384]{3,2,1,0:T(8,128)(2,1)S(1)}, bf16[2,2,160,384]{3,2,1,0:T(8,128)(2,1)}, u32[]{:S(2)}) copy-start(bf16[2,2,160,384]{3,2,1,0:T(8,128)(2,1)} %get-tuple-element.26) | copy-start | bytes 1474564
  133.2 5.5 %copy-start.18 = (bf16[2,2,160,384]{3,2,1,0:T(8,128)(2,1)S(1)}, bf16[2,2,160,384]{3,2,1,0:T(8,128)(2,1)}, u32[]{:S(2)}) copy-start(bf16[2,2,160,384]{3,2,1,0:T(8,128)(2,1)} %get-tuple-element.27) | copy-start | bytes 1474564
  136.2 3.4 copy-start.17
  137.8 2.3 copy-start.16
  138.7 2.3 copy-start.15
  139.2 2.3 copy-start.14
  140.1 2.3 copy-start.13
  140.6 2.3 copy-start.12
  141.5 2.4 copy-start.10
  142.0 2.4 copy-start.9
  142.5 3.3 copy-start.4
  142.9 4.3 copy-start.8
  143.4 5.2 %copy-start.7 = (bf16[2,2,160,384]{3,2,1,0:T(8,128)(2,1)S(1)}, bf16[2,2,160,384]{3,2,1,0:T(8,128)(2,1)}, u32[]{:S(2)}) copy-start(bf16[2,2,160,384]{3,2,1,0:T(8,128)(2,1)} %get-tuple-element.37) | copy-start | bytes 1474564
  143.9 6.1 %copy-start.6 = (bf16[2,2,160,384]{3,2,1,0:T(8,128)(2,1)S(1)}, bf16[2,2,160,384]{3,2,1,0:T(8,128)(2,1)}, u32[]{:S(2)}) copy-start(bf16[2,2,160,384]{3,2,1,0:T(8,128)(2,1)} %get-tuple-element.21) | copy-start | bytes 1474564
  144.4 7.1 %copy-start.5 = (bf16[2,2,160,384]{3,2,1,0:T(8,128)(2,1)S(1)}, bf16[2,2,160,384]{3,2,1,0:T(8,128)(2,1)}, u32[]{:S(2)}) copy-start(bf16[2,2,160,384]{3,2,1,0:T(8,128)(2,1)} %get-tuple-element.39) | copy-start | bytes 1474564
  152.9 5.6 %copy-start.20 = (f32[384]{0:T(512)S(1)}, f32[384]{0:T(512)}, u32[]{:S(2)}) copy-start(f32[384]{0:T(512)} %param.5) | copy-start | bytes 4612
  162.0 3.2 collective-permute-start.3
  165.3 10.8 %collective-permute-start.5 = (bf16[4,1,160,384]{3,2,1,0:T(8,128)(2,1)S(1)}, bf16[4,1,160,384]{3,2,1,0:T(8,128)(2,1)S(1)}, u32[]{:S(2)}, u32[]{:S(2)}) collective-permute-start(bf16[4,1,160,384]{3,2,1,0:T(8,128)(2,1)S(1)} %get-tuple-element.46), channel_id=1, source_target_pairs={{1,0},{2,1},{3,2},{5,4},{6,5},{7,6},{9,8},{10,9},{11,10},{13,12},{... | collective-permute-start | bytes 1474568 | tf_op jit(solution)/shard_map/ppermute | solution.py:23
  166.6 11.3 %collective-permute-start.4 = (bf16[4,1,160,384]{3,2,1,0:T(8,128)(2,1)S(1)}, bf16[4,1,160,384]{3,2,1,0:T(8,128)(2,1)S(1)}, u32[]{:S(2)}, u32[]{:S(2)}) collective-permute-start(bf16[4,1,160,384]{3,2,1,0:T(8,128)(2,1)S(1)} %get-tuple-element.45), channel_id=1, source_target_pairs={{0,1},{1,2},{2,3},{4,5},{5,6},{6,7},{8,9},{9,10},{10,11},{12,13},{... | collective-permute-start | bytes 1474568 | tf_op jit(solution)/shard_map/ppermute | solution.py:20
  214.6 243.6 %reduce-scatter.5.cloned.1.call-start = ((), (), s32[]{:S(2)}) async-start(), calls=%async_computation.4 | async-start | bytes 7077888 | tf_op jit(solution)/shard_map/reduce_scatter | solution.py:66
Sparse Core Ops, SparseCore 0:
  9.9 106.2 all-gather.1
  214.7 166.2 reduce-scatter.2
  387.3 70.8 reduce-scatter.4
where the time goes:
time: 468 us; the launch traced here: 467 us
  waiting for transfers between devices  297 us (63%)
  matrix products  65.9 us (14%)
  blocking collectives  41.3 us (9%)
  local copies, waits for them, and re-layouts  23.7 us (5%)
  starting transfers between devices  15.8 us (3%)
  between operations  14.3 us (3%)
  other arithmetic  9.04 us (2%)
    reduce_scatter x1, waiting for transfers between devices, shards(): lax.psum_scatter(jnp.stack(outputs, axis=1), 'height', scatter_dimension=...  166 us
    all_gather x1, waiting for transfers between devices, shards(): piece = lax.all_gather(kernel, 'height', axis=0, tiled=True)  77.1 us
    psum x1, blocking collectives, shards(): lax.psum((gain_local, bias_local), ('tm', 'height'))  41.3 us
    dot_general x27, matrix products, shards(): lax.dot_general(left, right, (((0,), (0,)), ((), ())), preferred_element_...  35.4 us
    dot_general x27, matrix products, shards(): lax.dot_general(grad_pad[2 - ktime:2 - ktime + frames, 2 - krow:2 - krow...  30.5 us
    reduce_scatter x1, waiting for transfers between devices, shards(): lax.psum_scatter(partial_rows, 'tm', scatter_dimension=2, tiled=True)  29 us
    ppermute x2, waiting for transfers between devices, padded(): lax.ppermute(lax.slice_in_dim(block, block.shape[dim] - width, None, axis...  11.4 us
    all_gather x1, local copies, waits for them, and re-layouts, shards(): piece = lax.all_gather(kernel, 'height', axis=0, tiled=True)  11.3 us
  transfers between devices with their start and end apart: 9, of which 9 were waited for; matrix products, arithmetic and copies ran while one was open for 2% of the time, Pallas kernels for 0%

commit v1 on v0

v1 whole, which is shorter than its diff:
```python
import functools
import math

import jax
import jax.numpy as jnp
from jax import lax
from jax.experimental import pallas as pl
from jax.experimental.pallas import tpu as pltpu
from jax.sharding import PartitionSpec as P

VMEM_BYTES = 56 * 1024 * 1024


def weight_grad_kernel(width, act_ref, cot_ref, out_ref):
    step = pl.program_id(0)
    ktime, krow = step // 3, step % 3
    own, _, cells = act_ref.shape
    start = pl.multiple_of((2 - krow) * width, 16)
    total = None
    for t in range(own):
        term = jnp.dot(
            act_ref[t],
            cot_ref[t + 2 - ktime, pl.ds(start, cells), :],
            preferred_element_type=jnp.float32,
        )
        total = term if total is None else total + term
    out_ref[0] = total


def weight_grad(act_taps, cot_ext, width):
    own, taps_in, cells = act_taps.shape
    chans = cot_ext.shape[-1]
    return pl.pallas_call(
        functools.partial(weight_grad_kernel, width),
        grid=(9,),
        out_shape=jax.ShapeDtypeStruct((9, taps_in, chans), jnp.float32),
        in_specs=[
            pl.BlockSpec(act_taps.shape, lambda j: (0, 0, 0)),
            pl.BlockSpec(cot_ext.shape, lambda j: (0, 0, 0)),
        ],
        out_specs=pl.BlockSpec((1, taps_in, chans), lambda j: (j, 0, 0)),
        compiler_params=pltpu.CompilerParams(vmem_limit_bytes=VMEM_BYTES),
        cost_estimate=pl.CostEstimate(
            flops=2 * 9 * own * taps_in * cells * chans, bytes_accessed=10**7, transcendentals=0
        ),
    )(act_taps, cot_ext)


def input_conv_kernel(width, cot_ref, kernel_ref, out_ref, total):
    frame, step = pl.program_id(0), pl.program_id(1)
    ktime, krow = step // 3, step % 3
    cells, wide = total.shape
    chans = cot_ref.shape[-1]
    part = wide // 3
    start = pl.multiple_of((2 - krow) * width, 16)
    rows = kernel_ref[...]
    weights = jnp.concatenate([rows[:, c * chans : (c + 1) * chans] for c in range(3)], axis=0)
    term = lax.dot_general(
        cot_ref[frame + 2 - ktime, pl.ds(start, cells), :],
        weights,
        (((1,), (1,)), ((), ())),
        preferred_element_type=jnp.float32,
    )

    @pl.when(step == 0)
    def _():
        total[...] = term

    @pl.when(step > 0)
    def _():
        total[...] += term

    @pl.when(step == 8)
    def _():
        column = lax.rem(lax.broadcasted_iota(jnp.int32, (cells, part), 0), width)
        sums = total[...]
        left = sums[:, :part]
        right = sums[:, 2 * part :]
        left = jnp.where(column == width - 1, 0.0, pltpu.roll(left, cells - 1, 0))
        right = jnp.where(column == 0, 0.0, pltpu.roll(right, 1, 0))
        out_ref[0] = left + sums[:, part : 2 * part] + right


def input_conv(cot_ext, kernel, own, width):
    cells = cot_ext.shape[1] - 2 * width
    chans = cot_ext.shape[2]
    part = kernel.shape[0]
    return pl.pallas_call(
        functools.partial(input_conv_kernel, width),
        grid=(own, 9),
        out_shape=jax.ShapeDtypeStruct((own, cells, part), jnp.float32),
        in_specs=[
            pl.BlockSpec(cot_ext.shape, lambda t, j: (0, 0, 0)),
            pl.BlockSpec((part, 3 * chans), lambda t, j: (0, j)),
        ],
        out_specs=pl.BlockSpec((1, cells, part), lambda t, j: (t, 0, 0)),
        scratch_shapes=[pltpu.VMEM((cells, 3 * part), jnp.float32)],
        compiler_params=pltpu.CompilerParams(vmem_limit_bytes=VMEM_BYTES),
        cost_estimate=pl.CostEstimate(
            flops=2 * own * 27 * cells * chans * part, bytes_accessed=10**7, transcendentals=0
        ),
    )(cot_ext, kernel)


def shards(block_input, gain, kernel, cotangent):
    frames, rows, width, chans = block_input.shape
    high = lax.axis_size("height")
    count = lax.axis_size("tm")
    part = chans // high
    total_rows = rows * high
    scale = 1.0 / math.sqrt(frames * count * total_rows * width)
    xfull = block_input.astype(jnp.float32)
    inv_rms = lax.rsqrt(jnp.mean(xfull * xfull, axis=-1, keepdims=True) + 1e-06)
    normed = xfull * inv_rms
    pre = normed * gain
    sig = jax.nn.sigmoid(pre)
    act = (pre * sig).astype(jnp.bfloat16)

    act_parts = act.reshape(frames, rows, width, high, part).transpose(3, 0, 1, 2, 4)
    act_all = lax.all_to_all(act_parts, "height", 0, 0, tiled=True)
    act_all = act_all.reshape(high, frames, rows, width, part).transpose(1, 0, 2, 3, 4)
    act_all = act_all.reshape(frames, total_rows, width, part)
    cot_all = lax.all_gather(cotangent, "height", axis=1, tiled=True)
    later = lax.ppermute(cot_all, "tm", [(i, i - 1) for i in range(1, count)])
    cot_ext = jnp.concatenate([cot_all, later], axis=0)
    cot_ext = jnp.pad(cot_ext, ((0, 0), (1, 1), (0, 0), (0, 0)))
    cot_ext = cot_ext.reshape(2 * frames, (total_rows + 2) * width, chans)

    act_pad = jnp.pad(act_all, ((0, 0), (0, 0), (1, 1), (0, 0)))
    act_taps = jnp.concatenate([act_pad[:, :, c : c + width] for c in range(3)], axis=-1)
    act_taps = act_taps.reshape(frames, total_rows * width, 3 * part).transpose(0, 2, 1)

    partial = weight_grad(act_taps, cot_ext, width)
    summed = lax.psum_scatter(partial, "tm", scatter_dimension=2, tiled=True)
    kernel_grad = summed.reshape(27, part, chans // count).transpose(1, 0, 2) * scale

    grads = input_conv(cot_ext, kernel, frames, width)
    grads = grads.reshape(frames, high, rows, width, part).transpose(1, 0, 2, 3, 4)
    grads = lax.all_to_all(grads, "height", 0, 0, tiled=True)
    act_grad = grads.transpose(1, 2, 3, 0, 4).reshape(frames, rows, width, chans)

    pre_grad = act_grad * sig * (1.0 + pre * (1.0 - sig))
    gain_local = jnp.sum(pre_grad * normed, axis=(0, 1, 2))
    bias_local = jnp.sum(cotangent.astype(jnp.float32), axis=(0, 1, 2))
    gain_total, bias_total = lax.psum((gain_local, bias_local), ("tm", "height"))
    normed_grad = pre_grad * gain
    input_grad = inv_rms * (
        normed_grad - normed * jnp.mean(normed_grad * normed, axis=-1, keepdims=True)
    )
    return (input_grad.astype(jnp.bfloat16), kernel_grad, gain_total * scale, bias_total * scale)


def solution(mesh):
    return jax.shard_map(
        shards,
        mesh=mesh,
        in_specs=(
            P("tm", "height", None, None),
            P(),
            P("height", None),
            P("tm", "height", None, None),
        ),
        out_specs=(P("tm", "height", None, None), P("height", None, "tm"), P(), P()),
        check_vma=False,
    )
```

time: 468 us -> 272 us (0.58)
  waiting for transfers between devices: 297 us -> 111 us
  matrix products: 65.9 us -> 0 us
  blocking collectives: 41.3 us -> 78.9 us
  Pallas kernels: 0 us -> 35 us
  starting transfers between devices: 15.8 us -> 4.9 us
  local copies, waits for them, and re-layouts: 23.7 us -> 17.2 us
    reduce_scatter x2 -> x1, waiting for transfers between devices: 195 us -> 56.6 us  [shards(): summed = lax.psum_scatter(partial, 'tm', scatter_dimension=2, tiled=True)]
    dot_general x54 -> x0, matrix products: 65.9 us -> none  [the longest x27 35.4 us: shards(): lax.dot_general(left, right, (((0,), (0,)), ((), ())), preferred_element_...]
    all_gather x1, waiting for transfers between devices: 77.1 us -> 38.9 us  [shards(): cot_all = lax.all_gather(cotangent, 'height', axis=1, tiled=True)]
    pallas_call x0 -> x2, Pallas kernels: none -> 35 us  [the longest x1 22.8 us: input_conv(): pl.pallas_call(functools.partial(input_conv_kernel, width), grid=(own, 9)...]
    psum x1, blocking collectives: 41.3 us -> 66.7 us  [shards(): lax.psum((gain_local, bias_local), ('tm', 'height'))]
    ppermute x6 -> x1, waiting for transfers between devices: 23.9 us -> 4.78 us  [shards(): later = lax.ppermute(cot_all, 'tm', [(i, i - 1) for i in range(1, count)])]
    ppermute x6 -> x1, starting transfers between devices: 15.7 us -> 1.28 us  [shards(): later = lax.ppermute(cot_all, 'tm', [(i, i - 1) for i in range(1, count)])]
    all_to_all x0 -> x1, blocking collectives: none -> 12.2 us  [shards(): act_all = lax.all_to_all(act_parts, 'height', 0, 0, tiled=True)]
  transfers between devices with their start and end apart: 9 -> 4, of which waited for: 9 -> 4; matrix products, arithmetic and copies ran while one was open for 2% -> 0% of each run, Pallas kernels for 0% -> 0%
where the time goes in v1:
time: 272 us; the launch traced here: 271 us
  waiting for transfers between devices  111 us (41%)
  blocking collectives  78.9 us (29%)
  Pallas kernels  35 us (13%)
  local copies, waits for them, and re-layouts  17.2 us (6%)
  between operations  14.2 us (5%)
  other arithmetic  9.87 us (4%)
  starting transfers between devices  4.9 us (2%)
    psum x1, blocking collectives, shards(): lax.psum((gain_local, bias_local), ('tm', 'height'))  66.7 us
    reduce_scatter x1, waiting for transfers between devices, shards(): summed = lax.psum_scatter(partial, 'tm', scatter_dimension=2, tiled=True)  56.6 us
    all_gather x1, waiting for transfers between devices, shards(): cot_all = lax.all_gather(cotangent, 'height', axis=1, tiled=True)  38.9 us
    pallas_call x1, Pallas kernels, input_conv(): pl.pallas_call(functools.partial(input_conv_kernel, width), grid=(own, 9)...  22.8 us
    pallas_call x1, Pallas kernels, weight_grad(): pl.pallas_call(functools.partial(weight_grad_kernel, width), grid=(9,), o...  12.2 us
    all_to_all x1, blocking collectives, shards(): act_all = lax.all_to_all(act_parts, 'height', 0, 0, tiled=True)  12.2 us
    all_to_all x1, waiting for transfers between devices, shards(): grads = lax.all_to_all(grads, 'height', 0, 0, tiled=True)  10.5 us
    pallas_call x1, local copies, waits for them, and re-layouts, weight_grad(): pl.pallas_call(functools.partial(weight_grad_kernel, width), grid=(9,), o...  8.97 us
  transfers between devices with their start and end apart: 4, of which 4 were waited for; matrix products, arithmetic and copies ran while one was open for 0% of the time, Pallas kernels for 0%

profile of v1, /device:TPU:0, one launch (start us, length us, event | category | flops | bytes accessed | tf_op | source)
XLA Modules:
  0.0 271.4 jit_solution(4752840027350441222)
XLA Ops:
  7.2 0.0 all-gather.2.cloned.1.call-start
  7.2 0.7 all-gather.2.cloned.1.call-update
  7.9 38.9 %all-gather.2.cloned.1.call-done = bf16[2,8,160,384]{3,2,1,0:T(8,128)(2,1)} async-done(((bf16[2,2,160,384]{3,2,1,0:T(8,128)(2,1)}), bf16[2,8,160,384]{3,2,1,0:T(8,128)(2,1)}) %all-gather.2.cloned.1.call-update) | async-done | bytes 1966096 | tf_op jit(solution)/shard_map/all_gather | solution.py:123
  46.8 1.3 collective-permute-start
  48.1 4.8 %collective-permute-done = bf16[2,8,160,384]{3,2,1,0:T(8,128)(2,1)S(1)} collective-permute-done((bf16[2,8,160,384]{3,2,1,0:T(8,128)(2,1)}, bf16[2,8,160,384]{3,2,1,0:T(8,128)(2,1)S(1)}, u32[]{:S(2)}, u32[]{:S(2)}) %collective-permute-start) | collective-permute-done | bytes 1966112 | tf_op jit(solution)/shard_map/ppermute | solution.py:124
  52.9 4.3 %fusion.3 = bf16[4,10,160,384]{3,2,1,0:T(8,128)(2,1)} fusion(bf16[2,8,160,384]{3,2,1,0:T(8,128)(2,1)S(1)} %collective-permute-done, bf16[2,8,160,384]{3,2,1,0:T(8,128)(2,1)} %all-gather.2.cloned.1.call-done), kind=kLoop, calls=%fused_computation.5 | loop fusion | flops 22118400 | bytes 8847360 | tf_op jit(solution)/shard_map/concatenate | solution.py:125
  57.1 22.8 %shard_map.75 = f32[2,1280,96]{2,1,0:T(8,128)} custom-call(bf16[4,1600,384]{2,1,0:T(8,128)(2,1)} %bitcast.24, bf16[96,10368]{1,0:T(8,128)(2,1)} %kernel_ref.1), custom_call_target="tpu_custom_call" | custom-call | flops 5096079360 | bytes 10000000 | tf_op jit(solution)/shard_map/pallas_call | solution.py:88
  79.9 0.0 copy-start
  79.9 2.5 copy.41
  82.5 3.5 %all-to-all-start = ((f32[4,2,2,160,96]{4,3,2,1,0:T(8,128)}), f32[4,2,2,160,96]{4,3,2,1,0:T(8,128)S(1)}, u32[]{:S(2)}, u32[]{:S(2)}) async-start(f32[4,2,2,160,96]{4,3,2,1,0:T(8,128)} %bitcast.20), calls=%async_computation | async-start | bytes 2621440 | tf_op jit(solution)/shard_map/all_to_all | solution.py:139
  86.0 0.0 reduce-scatter.2.cloned.1.call-start
  86.1 0.0 copy-done
  86.1 0.2 fusion.22
  86.3 10.5 %all-to-all-done = f32[4,2,2,160,96]{4,3,2,1,0:T(8,128)S(1)} async-done(((f32[4,2,2,160,96]{4,3,2,1,0:T(8,128)}), f32[4,2,2,160,96]{4,3,2,1,0:T(8,128)S(1)}, u32[]{:S(2)}, u32[]{:S(2)}) %all-to-all-start) | async-done | bytes 983072 | tf_op jit(solution)/shard_map/all_to_all | solution.py:139
  96.8 0.0 copy-start.2
  96.8 0.8 copy.32
  97.7 0.6 reshape.46
  98.3 0.0 copy-done.2
  98.3 0.8 fusion.21
  99.1 1.3 fusion.16
  100.4 0.5 reshape.47
  100.9 0.1 copy.33
  101.0 12.2 %all_to_all.10 = bf16[4,2,2,160,96]{4,3,2,1,0:T(8,128)(2,1)S(1)} all-to-all(bf16[4,2,2,160,96]{4,3,2,1,0:T(8,128)(2,1)S(1)} %copy.33), channel_id=1, replica_groups=mesh['tm'=8,'height'=4] {'height'}, dimensions={0} | all-to-all | bytes 983040 | tf_op jit(solution)/shard_map/all_to_all | solution.py:120
  113.2 0.3 pad_slice_fusion.1
  113.5 0.2 copy.37
  113.8 0.2 copy.36
  114.0 0.2 copy.35
  114.3 1.2 maximum_bitcast_fusion.act_ref
  115.5 12.2 %shard_map.76 = f32[9,288,384]{2,1,0:T(8,128)} custom-call(bf16[2,288,1280]{2,1,0:T(8,128)(2,1)} %maximum_bitcast_fusion.act_ref, bf16[4,1600,384]{2,1,0:T(8,128)(2,1)} %bitcast.25), custom_call_target="tpu_custom_call" | custom-call | flops 5096079360 | bytes 10000000 | tf_op jit(solution)/shard_map/pallas_call | solution.py:33
  127.7 9.0 %copy.38 = f32[9,288,384]{1,0,2:T(8,128)} copy(f32[9,288,384]{2,1,0:T(8,128)} %shard_map.76) | data formatting | bytes 7962624 | tf_op jit(solution)/shard_map/pallas_call | solution.py:33
  136.7 0.0 copy-start.1
  136.7 0.0 reduce-scatter.2.cloned.1.call-update
  136.7 1.0 copy-done.1
  137.7 0.1 convert_reduce_fusion
  137.8 66.7 %all-reduce.2 = (f32[384]{0:T(512)S(1)}, f32[384]{0:T(512)S(1)}) all-reduce(f32[384]{0:T(512)S(1)} %get-tuple-element.8, f32[384]{0:T(512)S(1)} %convert_reduce_fusion), channel_id=1, replica_groups=mesh['tm'=8,'height'=4] {'tm','height'}, use_global_device_ids=true, to_apply=%region_4.5 | all-reduce | flops 768 | bytes 6144 | tf_op jit(solution)/shard_map/psum | solution.py:145
  204.5 0.6 broadcast_multiply_fusion.2
  205.1 56.6 %reduce-scatter.2.cloned.1.call-done = f32[9,288,48]{1,0,2:T(8,128)} async-done(((f32[9,288,384]{1,0,2:T(8,128)}), f32[9,288,48]{1,0,2:T(8,128)}) %reduce-scatter.2.cloned.1.call-update) | async-done | bytes 497680 | tf_op jit(solution)/shard_map/reduce_scatter | solution.py:134
  261.7 1.4 broadcast_multiply_fusion
  263.1 0.3 mul.91
  263.4 1.2 copy.39
  (3 shorter events, 0.1 us)
Async XLA Ops:
  7.2 39.6 %all-gather.2.cloned.1.call-start = ((), (), s32[]{:S(2)}) async-start(), calls=%async_computation.3 | async-start | bytes 2457600 | tf_op jit(solution)/shard_map/all_gather | solution.py:123
  46.8 6.1 %collective-permute-start = (bf16[2,8,160,384]{3,2,1,0:T(8,128)(2,1)}, bf16[2,8,160,384]{3,2,1,0:T(8,128)(2,1)S(1)}, u32[]{:S(2)}, u32[]{:S(2)}) collective-permute-start(bf16[2,8,160,384]{3,2,1,0:T(8,128)(2,1)} %all-gather.2.cloned.1.call-done), channel_id=1, source_target_pairs={{4,0},{8,4},{12,8},{16,12},{20,16},{24,20},{28,24},{5,1},{9,5},{13... | collective-permute-start | bytes 5898248 | tf_op jit(solution)/shard_map/ppermute | solution.py:124
  79.9 6.1 %copy-start = (bf16[2,2,160,384]{3,2,1,0:T(8,128)(2,1)S(1)}, bf16[2,2,160,384]{3,2,1,0:T(8,128)(2,1)}, u32[]{:S(2)}) copy-start(bf16[2,2,160,384]{3,2,1,0:T(8,128)(2,1)} %param.4) | copy-start | bytes 1474564
  82.5 14.3 %all-to-all-start = ((f32[4,2,2,160,96]{4,3,2,1,0:T(8,128)}), f32[4,2,2,160,96]{4,3,2,1,0:T(8,128)S(1)}, u32[]{:S(2)}, u32[]{:S(2)}) async-start(f32[4,2,2,160,96]{4,3,2,1,0:T(8,128)} %bitcast.20), calls=%async_computation | async-start | bytes 2621440 | tf_op jit(solution)/shard_map/all_to_all | solution.py:139
  86.0 175.7 %reduce-scatter.2.cloned.1.call-start = ((), (), s32[]{:S(2)}) async-start(), calls=%async_computation.4 | async-start | bytes 10616832 | tf_op jit(solution)/shard_map/reduce_scatter | solution.py:134
  96.8 1.5 copy-start.2
  136.7 1.0 copy-start.1
Sparse Core Ops, SparseCore 0:
  9.8 36.9 all-gather.1
  136.8 124.8 reduce-scatter.1

commit v2 on v1

--- a/solution.py
+++ b/solution.py
@@ -9,6 +9,337 @@
 from jax.sharding import PartitionSpec as P
 
 VMEM_BYTES = 56 * 1024 * 1024
+MESH = pl.DeviceIdType.MESH
+
+
+def remote(source, target, send, receive, where):
+    return pltpu.make_async_remote_copy(
+        src_ref=source,
+        dst_ref=target,
+        send_sem=send,
+        recv_sem=receive,
+        device_id=where,
+        device_id_type=MESH,
+    )
+
+
+def at_place(tm, height):
+    return (tm, height)
+
+
+def exchange_kernel(
+    count, high, width, act_ref, cot_ref, act_all, cot_ext, zeros, local_sem, zero_sem,
+    act_send, act_recv, cot_send, cot_recv, halo_send, halo_recv,
+):
+    me, row = lax.axis_index("tm"), lax.axis_index("height")
+    frames, block, chans = cot_ref.shape
+    whole = high * block
+    has_prev, has_next = me > 0, me < count - 1
+    barrier = pltpu.get_barrier_semaphore()
+    for d in range(1, high):
+        pl.semaphore_signal(
+            barrier, inc=1, device_id=at_place(me, lax.rem(row + d, high)), device_id_type=MESH
+        )
+
+    for step in (1, count - 1):
+        pl.semaphore_signal(
+            barrier, inc=1, device_id=at_place(lax.rem(me + step, count), row), device_id_type=MESH
+        )
+    zeros[...] = jnp.zeros_like(zeros)
+    pl.semaphore_wait(barrier, high + 1)
+
+    def cot_slot(owner):
+        return pl.ds(pl.multiple_of(width + owner * block, 16), block)
+
+    def act_slot(owner):
+        return pl.ds(pl.multiple_of(owner * block, 16), block)
+
+    def cot_copy(f, d):
+        return remote(
+            cot_ref.at[f], cot_ext.at[f, cot_slot(row)],
+            cot_send.at[f, d], cot_recv.at[f, d], at_place(me, lax.rem(row + d, high)),
+        )
+
+    def halo_copy(f, d):
+        slot = cot_slot(lax.rem(row + high - d, high))
+        source = cot_ref.at[f] if d == 0 else cot_ext.at[f, slot]
+        return remote(
+            source, cot_ext.at[frames + f, slot],
+            halo_send.at[f, d], halo_recv.at[f, d], at_place(me - 1, row),
+        )
+
+    def act_copy(d):
+        peer = lax.rem(row + d, high)
+        return remote(
+            act_ref.at[peer], act_all.at[:, act_slot(row)],
+            act_send.at[d], act_recv.at[d], at_place(me, peer),
+        )
+
+    locals_ = [
+        pltpu.make_async_copy(act_ref.at[row], act_all.at[:, act_slot(row)], local_sem.at[frames])
+    ]
+    for f in range(frames):
+        locals_.append(
+            pltpu.make_async_copy(cot_ref.at[f], cot_ext.at[f, cot_slot(row)], local_sem.at[f])
+        )
+    edges = []
+    for f in range(2 * frames):
+        for side, start in enumerate((0, width + whole)):
+            edges.append(
+                pltpu.make_async_copy(
+                    zeros.at[pl.ds(0, width)], cot_ext.at[f, pl.ds(start, width)],
+                    zero_sem.at[2 * f + side],
+                )
+            )
+    fills = []
+    for f in range(frames):
+        for r in range(high):
+            fills.append(
+                pltpu.make_async_copy(
+                    zeros, cot_ext.at[frames + f, pl.ds(width + r * block, block)],
+                    halo_recv.at[f, r],
+                )
+            )
+
+    for f in range(frames):
+        for d in range(1, high):
+            cot_copy(f, d).start()
+
+        @pl.when(has_prev)
+        def _():
+            halo_copy(f, 0).start()
+
+    for d in range(1, high):
+        act_copy(d).start()
+    for copy in locals_ + edges:
+        copy.start()
+
+    @pl.when(me == count - 1)
+    def _():
+        for copy in fills:
+            copy.start()
+
+    for f in range(frames):
+        for d in range(1, high):
+            cot_copy(f, d).wait_recv()
+
+            @pl.when(has_prev)
+            def _():
+                halo_copy(f, d).start()
+
+    for copy in locals_ + edges:
+        copy.wait()
+    for d in range(1, high):
+        act_copy(d).wait()
+        for f in range(frames):
+            cot_copy(f, d).wait_send()
+
+    @pl.when(has_prev)
+    def _():
+        for f in range(frames):
+            for d in range(high):
+                halo_copy(f, d).wait_send()
+
+    @pl.when(has_next)
+    def _():
+        for f in range(frames):
+            for d in range(high):
+                halo_copy(f, d).wait_recv()
+
+    @pl.when(me == count - 1)
+    def _():
+        for copy in fills:
+            copy.wait()
+
+
+def exchange(act_parts, cot, width):
+    count, high = lax.axis_size("tm"), lax.axis_size("height")
+    frames, block, chans = cot.shape
+    part = act_parts.shape[-1]
+    anywhere = pl.BlockSpec(memory_space=pl.ANY)
+    dma = pltpu.SemaphoreType.DMA
+    return pl.pallas_call(
+        functools.partial(exchange_kernel, count, high, width),
+        out_shape=(
+            jax.ShapeDtypeStruct((frames, high * block, part), act_parts.dtype),
+            jax.ShapeDtypeStruct((2 * frames, high * block + 2 * width, chans), cot.dtype),
+        ),
+        in_specs=[anywhere, anywhere],
+        out_specs=(anywhere, anywhere),
+        scratch_shapes=[
+            pltpu.VMEM((block, chans), cot.dtype),
+            dma((frames + 1,)),
+            dma((4 * frames,)),
+            dma((high,)),
+            dma((high,)),
+            dma((frames, high)),
+            dma((frames, high)),
+            dma((frames, high)),
+            dma((frames, high)),
+        ],
+        compiler_params=pltpu.CompilerParams(collective_id=0, has_side_effects=True),
+    )(act_parts, cot)
+
+
+def combine_kernel(
+    chips, high, scale, partial_ref, grads_ref, out_ref, back_ref, pair_land, send_buf, recv_buf,
+    pair_send, pair_recv, chip_send, chip_recv, back_send, back_recv, local_sem,
+):
+    me, row = lax.axis_index("tm"), lax.axis_index("height")
+    chip, core = me // 2, lax.rem(me, 2)
+    block = back_ref.shape[2]
+    other = chip * 2 + 1 - core
+    barrier = pltpu.get_barrier_semaphore()
+    pl.semaphore_signal(barrier, inc=1, device_id=at_place(other, row), device_id_type=MESH)
+    for k in range(1, chips):
+        pl.semaphore_signal(
+            barrier, inc=1, device_id=at_place(lax.rem(chip + k, chips) * 2 + core, row),
+            device_id_type=MESH,
+        )
+    for d in range(1, high):
+        pl.semaphore_signal(
+            barrier, inc=1, device_id=at_place(me, lax.rem(row + d, high)), device_id_type=MESH
+        )
+    pl.semaphore_wait(barrier, chips + high - 1)
+
+    def pair_copy(k):
+        goal = lax.rem(chip + k, chips)
+        return remote(
+            partial_ref.at[goal * 2 + 1 - core], pair_land.at[k],
+            pair_send.at[k], pair_recv.at[k], at_place(other, row),
+        )
+
+    def chip_copy(k):
+        return remote(
+            send_buf.at[k - 1], recv_buf.at[k - 1], chip_send.at[k - 1], chip_recv.at[k - 1],
+            at_place(lax.rem(chip + k, chips) * 2 + core, row),
+        )
+
+    def part_of(owner):
+        return grads_ref.at[:, pl.ds(pl.multiple_of(owner * block, 16), block)]
+
+    def back_copy(d):
+        peer = lax.rem(row + d, high)
+        return remote(
+            part_of(peer), back_ref.at[row], back_send.at[d], back_recv.at[d], at_place(me, peer)
+        )
+
+    order = list(range(1, chips)) + [0]
+    for k in order:
+        pair_copy(k).start()
+    for d in range(1, high):
+        back_copy(d).start()
+    own = pltpu.make_async_copy(part_of(row), back_ref.at[row], local_sem)
+    own.start()
+    for k in range(1, chips):
+        pair_copy(k).wait_recv()
+        mine = lax.rem(chip + k, chips) * 2 + core
+        send_buf[k - 1] = (partial_ref[mine] + pair_land[k]).astype(send_buf.dtype)
+        chip_copy(k).start()
+    pair_copy(0).wait_recv()
+    out_ref[...] = partial_ref[me] + pair_land[0]
+    for k in range(1, chips):
+        chip_copy(k).wait_recv()
+        out_ref[...] += recv_buf[k - 1].astype(jnp.float32)
+    out_ref[...] *= scale
+    for k in order:
+        pair_copy(k).wait_send()
+    for k in range(1, chips):
+        chip_copy(k).wait_send()
+    for d in range(1, high):
+        back_copy(d).wait()
+    own.wait()
+
+
+def combine(partial, grads, rows_block, scale):
+    count, high = lax.axis_size("tm"), lax.axis_size("height")
+    chips = count // 2
+    frames, _, part = grads.shape
+    one = partial.shape[1:]
+    dma = pltpu.SemaphoreType.DMA
+    anywhere = pl.BlockSpec(memory_space=pl.ANY)
+    vmem = pl.BlockSpec(memory_space=pltpu.VMEM)
+    return pl.pallas_call(
+        functools.partial(combine_kernel, chips, high, scale),
+        out_shape=(
+            jax.ShapeDtypeStruct(one, jnp.float32),
+            jax.ShapeDtypeStruct((high, frames, rows_block, part), jnp.float32),
+        ),
+        in_specs=[vmem, anywhere],
+        out_specs=(vmem, anywhere),
+        scratch_shapes=[
+            pltpu.VMEM((chips,) + one, jnp.float32),
+            pltpu.VMEM((chips - 1,) + one, jnp.bfloat16),
+            pltpu.VMEM((chips - 1,) + one, jnp.bfloat16),
+            dma((chips,)),
+            dma((chips,)),
+            dma((chips - 1,)),
+            dma((chips - 1,)),
+            dma((high,)),
+            dma((high,)),
+            dma,
+        ],
+        compiler_params=pltpu.CompilerParams(
+            collective_id=1, has_side_effects=True, vmem_limit_bytes=VMEM_BYTES
+        ),
+    )(partial, grads)
+
+
+def stats_kernel(count, high, local_ref, out_ref, land, middle, across, ts, tr, hs, hr):
+    me, row = lax.axis_index("tm"), lax.axis_index("height")
+    barrier = pltpu.get_barrier_semaphore()
+    for d in range(1, count):
+        pl.semaphore_signal(
+            barrier, inc=1, device_id=at_place(lax.rem(me + d, count), row), device_id_type=MESH
+        )
+    for d in range(1, high):
+        pl.semaphore_signal(
+            barrier, inc=1, device_id=at_place(me, lax.rem(row + d, high)), device_id_type=MESH
+        )
+    pl.semaphore_wait(barrier, count + high - 2)
+
+    def first(d):
+        place = at_place(lax.rem(me + d, count), row)
+        return remote(local_ref, land.at[me], ts.at[d], tr.at[d], place)
+
+    def second(d):
+        place = at_place(me, lax.rem(row + d, high))
+        return remote(middle, across.at[row], hs.at[d], hr.at[d], place)
+
+    for d in range(1, count):
+        first(d).start()
+    land[me] = local_ref[...]
+    for d in range(1, count):
+        first(d).wait()
+    middle[...] = jnp.sum(land[...], axis=0)
+    for d in range(1, high):
+        second(d).start()
+    across[row] = middle[...]
+    for d in range(1, high):
+        second(d).wait()
+    out_ref[...] = jnp.sum(across[...], axis=0)
+
+
+def stats_sum(local):
+    count, high = lax.axis_size("tm"), lax.axis_size("height")
+    vmem = pl.BlockSpec(memory_space=pltpu.VMEM)
+    dma = pltpu.SemaphoreType.DMA
+    return pl.pallas_call(
+        functools.partial(stats_kernel, count, high),
+        out_shape=jax.ShapeDtypeStruct(local.shape, local.dtype),
+        in_specs=[vmem],
+        out_specs=vmem,
+        scratch_shapes=[
+            pltpu.VMEM((count,) + local.shape, local.dtype),
+            pltpu.VMEM(local.shape, local.dtype),
+            pltpu.VMEM((high,) + local.shape, local.dtype),
+            dma((count,)),
+            dma((count,)),
+            dma((high,)),
+            dma((high,)),
+        ],
+        compiler_params=pltpu.CompilerParams(collective_id=2, has_side_effects=True),
+    )(local)
 
 
 def weight_grad_kernel(width, act_ref, cot_ref, out_ref):
@@ -24,21 +355,21 @@
             preferred_element_type=jnp.float32,
         )
         total = term if total is None else total + term
-    out_ref[0] = total
-
-
-def weight_grad(act_taps, cot_ext, width):
+    out_ref[:, 0] = total.T.reshape(out_ref.shape[0], out_ref.shape[2], out_ref.shape[3])
+
+
+def weight_grad(act_taps, cot_ext, width, count):
     own, taps_in, cells = act_taps.shape
     chans = cot_ext.shape[-1]
     return pl.pallas_call(
         functools.partial(weight_grad_kernel, width),
         grid=(9,),
-        out_shape=jax.ShapeDtypeStruct((9, taps_in, chans), jnp.float32),
+        out_shape=jax.ShapeDtypeStruct((count, 9, chans // count, taps_in), jnp.float32),
         in_specs=[
             pl.BlockSpec(act_taps.shape, lambda j: (0, 0, 0)),
             pl.BlockSpec(cot_ext.shape, lambda j: (0, 0, 0)),
         ],
-        out_specs=pl.BlockSpec((1, taps_in, chans), lambda j: (j, 0, 0)),
+        out_specs=pl.BlockSpec((count, 1, chans // count, taps_in), lambda j: (0, j, 0, 0)),
         compiler_params=pltpu.CompilerParams(vmem_limit_bytes=VMEM_BYTES),
         cost_estimate=pl.CostEstimate(
             flops=2 * 9 * own * taps_in * cells * chans, bytes_accessed=10**7, transcendentals=0
@@ -117,37 +448,34 @@
     act = (pre * sig).astype(jnp.bfloat16)
 
     act_parts = act.reshape(frames, rows, width, high, part).transpose(3, 0, 1, 2, 4)
-    act_all = lax.all_to_all(act_parts, "height", 0, 0, tiled=True)
-    act_all = act_all.reshape(high, frames, rows, width, part).transpose(1, 0, 2, 3, 4)
+    act_parts = act_parts.reshape(high, frames, rows * width, part)
+    cot_flat = cotangent.reshape(frames, rows * width, chans)
+    act_all, cot_ext = exchange(act_parts, cot_flat, width)
     act_all = act_all.reshape(frames, total_rows, width, part)
-    cot_all = lax.all_gather(cotangent, "height", axis=1, tiled=True)
-    later = lax.ppermute(cot_all, "tm", [(i, i - 1) for i in range(1, count)])
-    cot_ext = jnp.concatenate([cot_all, later], axis=0)
-    cot_ext = jnp.pad(cot_ext, ((0, 0), (1, 1), (0, 0), (0, 0)))
-    cot_ext = cot_ext.reshape(2 * frames, (total_rows + 2) * width, chans)
 
     act_pad = jnp.pad(act_all, ((0, 0), (0, 0), (1, 1), (0, 0)))
     act_taps = jnp.concatenate([act_pad[:, :, c : c + width] for c in range(3)], axis=-1)
     act_taps = act_taps.reshape(frames, total_rows * width, 3 * part).transpose(0, 2, 1)
 
-    partial = weight_grad(act_taps, cot_ext, width)
-    summed = lax.psum_scatter(partial, "tm", scatter_dimension=2, tiled=True)
-    kernel_grad = summed.reshape(27, part, chans // count).transpose(1, 0, 2) * scale
-
+    partial = weight_grad(act_taps, cot_ext, width, count)
     grads = input_conv(cot_ext, kernel, frames, width)
-    grads = grads.reshape(frames, high, rows, width, part).transpose(1, 0, 2, 3, 4)
-    grads = lax.all_to_all(grads, "height", 0, 0, tiled=True)
-    act_grad = grads.transpose(1, 2, 3, 0, 4).reshape(frames, rows, width, chans)
+    summed, back = combine(partial, grads, rows * width, scale)
+    kernel_grad = summed.reshape(9, chans // count, 3, part).transpose(3, 0, 2, 1)
+    kernel_grad = kernel_grad.reshape(part, 27, chans // count)
+    act_grad = back.transpose(1, 2, 0, 3).reshape(frames, rows, width, chans)
 
     pre_grad = act_grad * sig * (1.0 + pre * (1.0 - sig))
     gain_local = jnp.sum(pre_grad * normed, axis=(0, 1, 2))
     bias_local = jnp.sum(cotangent.astype(jnp.float32), axis=(0, 1, 2))
-    gain_total, bias_total = lax.psum((gain_local, bias_local), ("tm", "height"))
+    local = jnp.concatenate(
+        [gain_local[None], bias_local[None], jnp.zeros((6, chans), jnp.float32)], axis=0
+    )
+    totals = stats_sum(local) * scale
     normed_grad = pre_grad * gain
     input_grad = inv_rms * (
         normed_grad - normed * jnp.mean(normed_grad * normed, axis=-1, keepdims=True)
     )
-    return (input_grad.astype(jnp.bfloat16), kernel_grad, gain_total * scale, bias_total * scale)
+    return (input_grad.astype(jnp.bfloat16), kernel_grad, totals[0], totals[1])
 
 
 def solution(mesh):

time: 272 us -> 138 us (0.51)
  waiting for transfers between devices: 111 us -> 0 us
  Pallas kernels: 35 us -> 121 us
  blocking collectives: 78.9 us -> 0 us
  between operations: 14.2 us -> 0.79 us
  local copies, waits for them, and re-layouts: 17.2 us -> 8.84 us
  starting transfers between devices: 4.9 us -> 0 us
    pallas_call x0 -> x3, Pallas kernels: none -> 84.3 us  [the longest x1 34.4 us: exchange(): pl.pallas_call(functools.partial(exchange_kernel, count, high, width), ou...]
    psum x1 -> x0, blocking collectives: 66.7 us -> none  [shards(): lax.psum((gain_local, bias_local), ('tm', 'height'))]
    reduce_scatter x1 -> x0, waiting for transfers between devices: 56.6 us -> none  [shards(): summed = lax.psum_scatter(partial, 'tm', scatter_dimension=2, tiled=True)]
    all_gather x1 -> x0, waiting for transfers between devices: 38.9 us -> none  [shards(): cot_all = lax.all_gather(cotangent, 'height', axis=1, tiled=True)]
    all_to_all x1 -> x0, blocking collectives: 12.2 us -> none  [shards(): act_all = lax.all_to_all(act_parts, 'height', 0, 0, tiled=True)]
    all_to_all x1 -> x0, waiting for transfers between devices: 10.5 us -> none  [shards(): grads = lax.all_to_all(grads, 'height', 0, 0, tiled=True)]
    pallas_call x1, local copies, waits for them, and re-layouts: 8.97 us -> 0.26 us  [exchange(): pl.pallas_call(functools.partial(exchange_kernel, count, high, width), ou...]
    ppermute x1 -> x0, waiting for transfers between devices: 4.78 us -> none  [shards(): later = lax.ppermute(cot_all, 'tm', [(i, i - 1) for i in range(1, count)])]
  transfers between devices with their start and end apart: 4 -> 0, of which waited for: 4 -> 0; matrix products, arithmetic and copies ran while one was open for 0% -> 0% of each run, Pallas kernels for 0% -> 0%
where the time goes in v2:
time: 138 us
  Pallas kernels  121 us (88%)
  local copies, waits for them, and re-layouts  8.84 us (6%)
  other arithmetic  7.27 us (5%)
    pallas_call x1, Pallas kernels, exchange(): pl.pallas_call(functools.partial(exchange_kernel, count, high, width), ou...  34.4 us
    pallas_call x1, Pallas kernels, combine(): pl.pallas_call(functools.partial(combine_kernel, chips, high, scale), out...  33.6 us
    pallas_call x1, Pallas kernels, input_conv(): pl.pallas_call(functools.partial(input_conv_kernel, width), grid=(own, 9)...  22.8 us
    pallas_call x1, Pallas kernels, stats_sum(): pl.pallas_call(functools.partial(stats_kernel, count, high), out_shape=ja...  16.3 us
    pallas_call x1, Pallas kernels, weight_grad(): pl.pallas_call(functools.partial(weight_grad_kernel, width), grid=(9,), o...  13.7 us

profile of v2, /device:TPU:0, one launch (start us, length us, event | category | flops | bytes accessed | tf_op | source)
XLA Modules:
  0.0 137.7 jit_solution(17957582007703588004)
XLA Ops:
  0.6 1.3 fusion.18
  1.9 1.4 %fusion.10 = bf16[2,2,160,384]{3,2,1,0:T(8,128)(2,1)S(1)} fusion(bf16[2,2,160,384]{3,2,1,0:T(8,128)(2,1)} %param.4, f32[384]{0:T(512)} %param.5, f32[2,2,160]{2,1,0:T(2,128)S(1)} %add_rsqrt_fusion), kind=kLoop, calls=%fused_computation.13 | loop fusion | flops 1966080 | bytes 987136 | tf_op jit(solution)/shard_map/convert_element_type | solution.py:448
  3.3 0.5 reshape.47
  3.8 0.9 copy.17
  4.7 34.4 %shard_map.75 = (bf16[2,1280,96]{2,1,0:T(8,128)(2,1)}, bf16[4,1600,384]{2,1,0:T(8,128)(2,1)}) custom-call(bf16[4,2,320,96]{3,2,1,0:T(8,128)(2,1)} %bitcast.15, bf16[2,320,384]{2,1,0:T(8,128)(2,1)} %bitcast.19), custom_call_target="tpu_custom_call" | custom-call | tf_op jit(solution)/shard_map/pallas_call | solution.py:161
  39.2 0.0 copy-start.1
  39.2 1.8 %pad_slice_fusion.1 = (bf16[2,8,160,96]{3,2,1,0:T(8,128)(2,1)S(1)}, bf16[2,8,160,96]{3,2,1,0:T(8,128)(2,1)S(1)}) fusion(bf16[2,8,160,96]{3,2,1,0:T(8,128)(2,1)} %bitcast.16), kind=kLoop, calls=%fused_computation.24 | loop fusion | bytes 1474560 | tf_op jit(solution)/shard_map/slice | solution.py:457
  41.0 0.3 copy.18
  41.2 0.3 copy.20
  41.5 0.0 copy-done.1
  41.5 0.3 copy.19
  41.8 1.2 maximum_bitcast_fusion.act_ref
  43.0 13.7 %shard_map.76.partial_ref = f32[8,9,48,288]{3,2,1,0:T(8,128)} custom-call(bf16[2,288,1280]{2,1,0:T(8,128)(2,1)} %maximum_bitcast_fusion.act_ref, bf16[4,1600,384]{2,1,0:T(8,128)(2,1)} %get-tuple-element.9.cot_ref), custom_call_target="tpu_custom_call" | custom-call | flops 5096079360 | bytes 10000000 | tf_op jit(solution)/shard_map/pallas_call | solution.py:364
  56.7 22.8 %shard_map.77.grads_ref = f32[2,1280,96]{2,1,0:T(8,128)} custom-call(bf16[4,1600,384]{2,1,0:T(8,128)(2,1)} %get-tuple-element.9.cot_ref, bf16[96,10368]{1,0:T(8,128)(2,1)} %kernel_ref.1), custom_call_target="tpu_custom_call" | custom-call | flops 5096079360 | bytes 10000000 | tf_op jit(solution)/shard_map/pallas_call | solution.py:419
  79.5 33.6 %shard_map.78 = (f32[9,48,288]{2,1,0:T(8,128)}, f32[4,2,320,96]{3,2,1,0:T(8,128)}) custom-call(f32[8,9,48,288]{3,2,1,0:T(8,128)} %shard_map.76.partial_ref, f32[2,1280,96]{2,1,0:T(8,128)} %shard_map.77.grads_ref), custom_call_target="tpu_custom_call" | custom-call | tf_op jit(solution)/shard_map/pallas_call | solution.py:262
  113.1 0.0 copy-start
  113.1 0.0 copy-start.4
  113.1 2.2 %copy.21 = f32[2,320,4,96]{3,2,1,0:T(4,128)S(1)} copy(f32[2,320,4,96]{3,1,0,2:T(8,128)} %bitcast.20) | data formatting | bytes 1966080 | tf_op jit(solution)/shard_map/transpose | solution.py:465
  115.3 0.6 reshape.51
  116.0 0.0 copy-done
  116.0 0.0 copy-done.4
  116.0 0.0 copy-start.2
  116.0 0.0 copy-start.3
  116.0 0.8 fusion.17
  116.8 1.1 fusion.16
  117.9 0.0 copy-done.2
  117.9 0.1 convert_reduce_fusion
  118.1 0.1 pad.7.clone
  118.1 0.7 maximum_maximum_fusion.local_ref
  118.8 16.3 %shard_map.79 = f32[8,384]{1,0:T(8,128)} custom-call(f32[8,384]{1,0:T(8,128)} %maximum_maximum_fusion.local_ref), custom_call_target="tpu_custom_call" | custom-call | tf_op jit(solution)/shard_map/pallas_call | solution.py:327
  135.1 0.7 broadcast_multiply_fusion
  135.8 0.6 slice_reduce_fusion
  136.4 0.0 copy-done.3
  136.4 0.4 reshape.52
  136.9 0.9 copy.22
  (5 shorter events, 0.0 us)
Async XLA Ops:
  39.2 2.3 %copy-start.1 = (bf16[2,1280,96]{2,1,0:T(8,128)(2,1)S(1)}, bf16[2,1280,96]{2,1,0:T(8,128)(2,1)}, u32[]{:S(2)}) copy-start(bf16[2,1280,96]{2,1,0:T(8,128)(2,1)} %get-tuple-element.8) | copy-start | bytes 1474564
  113.1 2.9 %copy-start = (bf16[2,2,160,384]{3,2,1,0:T(8,128)(2,1)S(1)}, bf16[2,2,160,384]{3,2,1,0:T(8,128)(2,1)}, u32[]{:S(2)}) copy-start(bf16[2,2,160,384]{3,2,1,0:T(8,128)(2,1)} %param.4) | copy-start | bytes 1474564
  113.1 2.9 %copy-start.4 = (f32[384]{0:T(512)S(1)}, f32[384]{0:T(512)}, u32[]{:S(2)}) copy-start(f32[384]{0:T(512)} %param.5) | copy-start | bytes 4612
  116.0 1.9 %copy-start.2 = (bf16[2,2,160,384]{3,2,1,0:T(8,128)(2,1)S(1)}, bf16[2,2,160,384]{3,2,1,0:T(8,128)(2,1)}, u32[]{:S(2)}) copy-start(bf16[2,2,160,384]{3,2,1,0:T(8,128)(2,1)} %param.7) | copy-start | bytes 1474564
  116.0 20.4 %copy-start.3 = (f32[9,48,288]{2,1,0:T(8,128)S(1)}, f32[9,48,288]{2,1,0:T(8,128)}, u32[]{:S(2)}) copy-start(f32[9,48,288]{2,1,0:T(8,128)} %get-tuple-element.11) | copy-start | bytes 1492996

commit v3 on v2

--- a/solution.py
+++ b/solution.py
@@ -181,26 +181,29 @@
     )(act_parts, cot)
 
 
-def combine_kernel(
-    chips, high, scale, partial_ref, grads_ref, out_ref, back_ref, pair_land, send_buf, recv_buf,
-    pair_send, pair_recv, chip_send, chip_recv, back_send, back_recv, local_sem,
+def finish_kernel(
+    count, high, width, scale, partial_ref, cot_ref, kernel_ref, input_ref, gain_ref, bias_ref,
+    out_ref, grad_ref, stats_ref,
+    weights, grads, back, pair_land, send_buf, recv_buf, local, land, middle, across,
+    pair_send, pair_recv, chip_send, chip_recv, back_send, back_recv, ts, tr, hs, hr,
 ):
     me, row = lax.axis_index("tm"), lax.axis_index("height")
     chip, core = me // 2, lax.rem(me, 2)
-    block = back_ref.shape[2]
+    chips = count // 2
+    _, frames, block, part = back.shape
+    cells = high * block
+    chans = cot_ref.shape[-1]
     other = chip * 2 + 1 - core
     barrier = pltpu.get_barrier_semaphore()
-    pl.semaphore_signal(barrier, inc=1, device_id=at_place(other, row), device_id_type=MESH)
-    for k in range(1, chips):
+    for d in range(1, count):
         pl.semaphore_signal(
-            barrier, inc=1, device_id=at_place(lax.rem(chip + k, chips) * 2 + core, row),
-            device_id_type=MESH,
+            barrier, inc=1, device_id=at_place(lax.rem(me + d, count), row), device_id_type=MESH
         )
     for d in range(1, high):
         pl.semaphore_signal(
             barrier, inc=1, device_id=at_place(me, lax.rem(row + d, high)), device_id_type=MESH
         )
-    pl.semaphore_wait(barrier, chips + high - 1)
+    pl.semaphore_wait(barrier, count + high - 2)
 
     def pair_copy(k):
         goal = lax.rem(chip + k, chips)
@@ -215,131 +218,180 @@
             at_place(lax.rem(chip + k, chips) * 2 + core, row),
         )
 
-    def part_of(owner):
-        return grads_ref.at[:, pl.ds(pl.multiple_of(owner * block, 16), block)]
-
-    def back_copy(d):
+    def part_of(f, owner):
+        return grads.at[f, pl.ds(pl.multiple_of(owner * block, 16), block)]
+
+    def back_copy(f, d):
         peer = lax.rem(row + d, high)
         return remote(
-            part_of(peer), back_ref.at[row], back_send.at[d], back_recv.at[d], at_place(me, peer)
-        )
+            part_of(f, peer), back.at[row, f], back_send.at[f, d], back_recv.at[f, d],
+            at_place(me, peer),
+        )
+
+    def first(d):
+        place = at_place(lax.rem(me + d, count), row)
+        return remote(local, land.at[me], ts.at[d], tr.at[d], place)
+
+    def second(d):
+        place = at_place(me, lax.rem(row + d, high))
+        return remote(middle, across.at[row], hs.at[d], hr.at[d], place)
 
     order = list(range(1, chips)) + [0]
     for k in order:
         pair_copy(k).start()
-    for d in range(1, high):
-        back_copy(d).start()
-    own = pltpu.make_async_copy(part_of(row), back_ref.at[row], local_sem)
-    own.start()
-    for k in range(1, chips):
-        pair_copy(k).wait_recv()
-        mine = lax.rem(chip + k, chips) * 2 + core
-        send_buf[k - 1] = (partial_ref[mine] + pair_land[k]).astype(send_buf.dtype)
-        chip_copy(k).start()
-    pair_copy(0).wait_recv()
-    out_ref[...] = partial_ref[me] + pair_land[0]
+    for j in range(9):
+        taps = [
+            kernel_ref[:, (3 * j + c) * chans : (3 * j + c + 1) * chans] for c in range(3)
+        ]
+        weights[:, j * chans : (j + 1) * chans] = jnp.concatenate(taps, axis=0)
+
+    span = 2 * block
+
+    def conv(f):
+        def body(step, carry):
+            left = jnp.concatenate(
+                [
+                    cot_ref[
+                        f + 2 - j // 3,
+                        pl.ds(pl.multiple_of(step * span + (2 - j % 3) * width, 16), span),
+                        :,
+                    ]
+                    for j in range(9)
+                ],
+                axis=1,
+            )
+            sums = lax.dot_general(
+                left, weights[...], (((1,), (1,)), ((), ())), preferred_element_type=jnp.float32
+            )
+            column = lax.rem(lax.broadcasted_iota(jnp.int32, (span, part), 0), width)
+            before = pltpu.roll(sums[:, :part], span - 1, 0)
+            after = pltpu.roll(sums[:, 2 * part :], 1, 0)
+            grads[f, pl.ds(pl.multiple_of(step * span, 16), span), :] = (
+                jnp.where(column == width - 1, 0.0, before)
+                + sums[:, part : 2 * part]
+                + jnp.where(column == 0, 0.0, after)
+            )
+            return carry
+
+        lax.fori_loop(0, cells // span, body, 0)
+        for d in range(1, high):
+            back_copy(f, d).start()
+        back[row, f] = part_of(f, row)[...]
+
+    for f in range(frames):
+        conv(f)
+        if f == 0:
+            for k in range(1, chips):
+                pair_copy(k).wait_recv()
+                mine = lax.rem(chip + k, chips) * 2 + core
+                send_buf[k - 1] = (partial_ref[mine] + pair_land[k]).astype(send_buf.dtype)
+                chip_copy(k).start()
+            pair_copy(0).wait_recv()
+            out_ref[...] = partial_ref[me] + pair_land[0]
+    for f in range(frames):
+        for d in range(1, high):
+            back_copy(f, d).wait_recv()
+
+    for f in range(frames):
+        wide = high * part
+        squares = 0.0
+        for h in range(high):
+            value = input_ref[h, f].astype(jnp.float32)
+            squares = squares + jnp.sum(value * value, axis=-1, keepdims=True)
+        inv_rms = lax.rsqrt(squares / wide + 1e-06)
+        inner = 0.0
+        for h in range(high):
+            normed = input_ref[h, f].astype(jnp.float32) * inv_rms
+            pre = normed * gain_ref[h]
+            sig = jax.nn.sigmoid(pre)
+            pre_grad = back[h, f] * sig * (1.0 + pre * (1.0 - sig))
+            product = pre_grad * normed
+            amount = jnp.sum(product, axis=0, keepdims=True)
+            if f == 0:
+                local[0, h] = amount
+            else:
+                local[0, h] += amount
+            normed_grad = pre_grad * gain_ref[h]
+            inner = inner + jnp.sum(normed_grad * normed, axis=-1, keepdims=True)
+            back[h, f] = normed_grad
+        if f == frames - 1:
+            local[1] = bias_ref[...]
+            for d in range(1, count):
+                first(d).start()
+            land[me] = local[...]
+        inner = inner / wide
+        for h in range(high):
+            normed = input_ref[h, f].astype(jnp.float32) * inv_rms
+            grad_ref[h, f] = (inv_rms * (back[h, f] - normed * inner)).astype(grad_ref.dtype)
+    for d in range(1, count):
+        first(d).wait_recv()
+    middle[...] = jnp.sum(land[...], axis=0)
+    for d in range(1, high):
+        second(d).start()
+    across[row] = middle[...]
     for k in range(1, chips):
         chip_copy(k).wait_recv()
         out_ref[...] += recv_buf[k - 1].astype(jnp.float32)
     out_ref[...] *= scale
+    for d in range(1, high):
+        second(d).wait_recv()
+    stats_ref[...] = jnp.sum(across[...], axis=0) * scale
     for k in order:
         pair_copy(k).wait_send()
     for k in range(1, chips):
         chip_copy(k).wait_send()
-    for d in range(1, high):
-        back_copy(d).wait()
-    own.wait()
-
-
-def combine(partial, grads, rows_block, scale):
+    for d in range(1, count):
+        first(d).wait_send()
+    for d in range(1, high):
+        second(d).wait_send()
+        for f in range(frames):
+            back_copy(f, d).wait_send()
+
+
+def finish(partial, cot_ext, kernel, inputs, gain, bias, width, scale):
     count, high = lax.axis_size("tm"), lax.axis_size("height")
     chips = count // 2
-    frames, _, part = grads.shape
+    _, frames, block, part = inputs.shape
+    chans = cot_ext.shape[-1]
     one = partial.shape[1:]
+    stats = (2,) + bias.shape
     dma = pltpu.SemaphoreType.DMA
-    anywhere = pl.BlockSpec(memory_space=pl.ANY)
     vmem = pl.BlockSpec(memory_space=pltpu.VMEM)
     return pl.pallas_call(
-        functools.partial(combine_kernel, chips, high, scale),
+        functools.partial(finish_kernel, count, high, width, scale),
         out_shape=(
             jax.ShapeDtypeStruct(one, jnp.float32),
-            jax.ShapeDtypeStruct((high, frames, rows_block, part), jnp.float32),
+            jax.ShapeDtypeStruct(inputs.shape, jnp.bfloat16),
+            jax.ShapeDtypeStruct(stats, jnp.float32),
         ),
-        in_specs=[vmem, anywhere],
-        out_specs=(vmem, anywhere),
+        in_specs=[vmem] * 6,
+        out_specs=(vmem,) * 3,
         scratch_shapes=[
+            pltpu.VMEM((3 * part, 9 * chans), jnp.bfloat16),
+            pltpu.VMEM((frames, high * block, part), jnp.float32),
+            pltpu.VMEM((high, frames, block, part), jnp.float32),
             pltpu.VMEM((chips,) + one, jnp.float32),
             pltpu.VMEM((chips - 1,) + one, jnp.bfloat16),
             pltpu.VMEM((chips - 1,) + one, jnp.bfloat16),
+            pltpu.VMEM(stats, jnp.float32),
+            pltpu.VMEM((count,) + stats, jnp.float32),
+            pltpu.VMEM(stats, jnp.float32),
+            pltpu.VMEM((high,) + stats, jnp.float32),
             dma((chips,)),
             dma((chips,)),
             dma((chips - 1,)),
             dma((chips - 1,)),
-            dma((high,)),
-            dma((high,)),
-            dma,
-        ],
-        compiler_params=pltpu.CompilerParams(
-            collective_id=1, has_side_effects=True, vmem_limit_bytes=VMEM_BYTES
-        ),
-    )(partial, grads)
-
-
-def stats_kernel(count, high, local_ref, out_ref, land, middle, across, ts, tr, hs, hr):
-    me, row = lax.axis_index("tm"), lax.axis_index("height")
-    barrier = pltpu.get_barrier_semaphore()
-    for d in range(1, count):
-        pl.semaphore_signal(
-            barrier, inc=1, device_id=at_place(lax.rem(me + d, count), row), device_id_type=MESH
-        )
-    for d in range(1, high):
-        pl.semaphore_signal(
-            barrier, inc=1, device_id=at_place(me, lax.rem(row + d, high)), device_id_type=MESH
-        )
-    pl.semaphore_wait(barrier, count + high - 2)
-
-    def first(d):
-        place = at_place(lax.rem(me + d, count), row)
-        return remote(local_ref, land.at[me], ts.at[d], tr.at[d], place)
-
-    def second(d):
-        place = at_place(me, lax.rem(row + d, high))
-        return remote(middle, across.at[row], hs.at[d], hr.at[d], place)
-
-    for d in range(1, count):
-        first(d).start()
-    land[me] = local_ref[...]
-    for d in range(1, count):
-        first(d).wait()
-    middle[...] = jnp.sum(land[...], axis=0)
-    for d in range(1, high):
-        second(d).start()
-    across[row] = middle[...]
-    for d in range(1, high):
-        second(d).wait()
-    out_ref[...] = jnp.sum(across[...], axis=0)
-
-
-def stats_sum(local):
-    count, high = lax.axis_size("tm"), lax.axis_size("height")
-    vmem = pl.BlockSpec(memory_space=pltpu.VMEM)
-    dma = pltpu.SemaphoreType.DMA
-    return pl.pallas_call(
-        functools.partial(stats_kernel, count, high),
-        out_shape=jax.ShapeDtypeStruct(local.shape, local.dtype),
-        in_specs=[vmem],
-        out_specs=vmem,
-        scratch_shapes=[
-            pltpu.VMEM((count,) + local.shape, local.dtype),
-            pltpu.VMEM(local.shape, local.dtype),
-            pltpu.VMEM((high,) + local.shape, local.dtype),
+            dma((frames, high)),
+            dma((frames, high)),
             dma((count,)),
             dma((count,)),
             dma((high,)),
             dma((high,)),
         ],
-        compiler_params=pltpu.CompilerParams(collective_id=2, has_side_effects=True),
-    )(local)
+        compiler_params=pltpu.CompilerParams(
+            collective_id=1, has_side_effects=True, vmem_limit_bytes=VMEM_BYTES
+        ),
+    )(partial, cot_ext, kernel, inputs, gain, bias)
 
 
 def weight_grad_kernel(width, act_ref, cot_ref, out_ref):
@@ -377,62 +429,6 @@
     )(act_taps, cot_ext)
 
 
-def input_conv_kernel(width, cot_ref, kernel_ref, out_ref, total):
-    frame, step = pl.program_id(0), pl.program_id(1)
-    ktime, krow = step // 3, step % 3
-    cells, wide = total.shape
-    chans = cot_ref.shape[-1]
-    part = wide // 3
-    start = pl.multiple_of((2 - krow) * width, 16)
-    rows = kernel_ref[...]
-    weights = jnp.concatenate([rows[:, c * chans : (c + 1) * chans] for c in range(3)], axis=0)
-    term = lax.dot_general(
-        cot_ref[frame + 2 - ktime, pl.ds(start, cells), :],
-        weights,
-        (((1,), (1,)), ((), ())),
-        preferred_element_type=jnp.float32,
-    )
-
-    @pl.when(step == 0)
-    def _():
-        total[...] = term
-
-    @pl.when(step > 0)
-    def _():
-        total[...] += term
-
-    @pl.when(step == 8)
-    def _():
-        column = lax.rem(lax.broadcasted_iota(jnp.int32, (cells, part), 0), width)
-        sums = total[...]
-        left = sums[:, :part]
-        right = sums[:, 2 * part :]
-        left = jnp.where(column == width - 1, 0.0, pltpu.roll(left, cells - 1, 0))
-        right = jnp.where(column == 0, 0.0, pltpu.roll(right, 1, 0))
-        out_ref[0] = left + sums[:, part : 2 * part] + right
-
-
-def input_conv(cot_ext, kernel, own, width):
-    cells = cot_ext.shape[1] - 2 * width
-    chans = cot_ext.shape[2]
-    part = kernel.shape[0]
-    return pl.pallas_call(
-        functools.partial(input_conv_kernel, width),
-        grid=(own, 9),
-        out_shape=jax.ShapeDtypeStruct((own, cells, part), jnp.float32),
-        in_specs=[
-            pl.BlockSpec(cot_ext.shape, lambda t, j: (0, 0, 0)),
-            pl.BlockSpec((part, 3 * chans), lambda t, j: (0, j)),
-        ],
-        out_specs=pl.BlockSpec((1, cells, part), lambda t, j: (t, 0, 0)),
-        scratch_shapes=[pltpu.VMEM((cells, 3 * part), jnp.float32)],
-        compiler_params=pltpu.CompilerParams(vmem_limit_bytes=VMEM_BYTES),
-        cost_estimate=pl.CostEstimate(
-            flops=2 * own * 27 * cells * chans * part, bytes_accessed=10**7, transcendentals=0
-        ),
-    )(cot_ext, kernel)
-
-
 def shards(block_input, gain, kernel, cotangent):
     frames, rows, width, chans = block_input.shape
     high = lax.axis_size("height")
@@ -458,24 +454,16 @@
     act_taps = act_taps.reshape(frames, total_rows * width, 3 * part).transpose(0, 2, 1)
 
     partial = weight_grad(act_taps, cot_ext, width, count)
-    grads = input_conv(cot_ext, kernel, frames, width)
-    summed, back = combine(partial, grads, rows * width, scale)
+    bias = jnp.sum(cotangent.astype(jnp.float32), axis=(0, 1, 2)).reshape(high, 1, part)
+    inputs = block_input.reshape(frames, rows * width, high, part).transpose(2, 0, 1, 3)
+    summed, grads, totals = finish(
+        partial, cot_ext, kernel, inputs, gain.reshape(high, 1, part), bias, width, scale
+    )
     kernel_grad = summed.reshape(9, chans // count, 3, part).transpose(3, 0, 2, 1)
     kernel_grad = kernel_grad.reshape(part, 27, chans // count)
-    act_grad = back.transpose(1, 2, 0, 3).reshape(frames, rows, width, chans)
-
-    pre_grad = act_grad * sig * (1.0 + pre * (1.0 - sig))
-    gain_local = jnp.sum(pre_grad * normed, axis=(0, 1, 2))
-    bias_local = jnp.sum(cotangent.astype(jnp.float32), axis=(0, 1, 2))
-    local = jnp.concatenate(
-        [gain_local[None], bias_local[None], jnp.zeros((6, chans), jnp.float32)], axis=0
-    )
-    totals = stats_sum(local) * scale
-    normed_grad = pre_grad * gain
-    input_grad = inv_rms * (
-        normed_grad - normed * jnp.mean(normed_grad * normed, axis=-1, keepdims=True)
-    )
-    return (input_grad.astype(jnp.bfloat16), kernel_grad, totals[0], totals[1])
+    input_grad = grads.transpose(1, 2, 0, 3).reshape(frames, rows, width, chans)
+    totals = totals.reshape(2, chans)
+    return (input_grad, kernel_grad, totals[0], totals[1])
 
 
 def solution(mesh):

time: 138 us -> 116 us (0.84)
  Pallas kernels: 121 us -> 98.3 us
  local copies, waits for them, and re-layouts: 8.84 us -> 13 us
  other arithmetic: 7.27 us -> 3.98 us
    pallas_call x3 -> x1, Pallas kernels: 72.7 us -> 50 us  [finish(): pl.pallas_call(functools.partial(finish_kernel, count, high, width, scale...]
    reshape x1 -> x5, local copies, waits for them, and re-layouts: 0.63 us -> 3.98 us  [the longest x2 1.43 us: shards(): block_input.reshape(frames, rows * width, high, part).transpose(2, 0, 1, 3)]
    transpose x1, local copies, waits for them, and re-layouts: 2.22 us -> 0.51 us  [shards(): input_grad = grads.transpose(1, 2, 0, 3).reshape(frames, rows, width, chans)]
where the time goes in v3:
time: 116 us
  Pallas kernels  98.3 us (85%)
  local copies, waits for them, and re-layouts  13 us (11%)
  other arithmetic  3.98 us (3%)
    pallas_call x1, Pallas kernels, finish(): pl.pallas_call(functools.partial(finish_kernel, count, high, width, scale...  50 us
    pallas_call x1, Pallas kernels, exchange(): pl.pallas_call(functools.partial(exchange_kernel, count, high, width), ou...  34.4 us
    pallas_call x1, Pallas kernels, weight_grad(): pl.pallas_call(functools.partial(weight_grad_kernel, width), grid=(9,), o...  13.8 us

profile of v3, /device:TPU:0, one launch (start us, length us, event | category | flops | bytes accessed | tf_op | source)
XLA Modules:
  0.0 116.0 jit_solution(3343714240896651584)
XLA Ops:
  0.6 1.3 %fusion = f32[2,2,160]{2,1,0:T(2,128)S(1)} fusion(bf16[2,2,160,384]{3,2,1,0:T(8,128)(2,1)} %param.4), kind=kLoop, calls=%fused_computation.3 | loop fusion | flops 736640 | bytes 494080 | tf_op jit(solution)/shard_map/reduce_sum | solution.py:440
  1.9 1.4 %fusion.7 = bf16[2,2,160,384]{3,2,1,0:T(8,128)(2,1)S(1)} fusion(bf16[2,2,160,384]{3,2,1,0:T(8,128)(2,1)} %param.4, f32[384]{0:T(512)} %param.5, f32[2,2,160]{2,1,0:T(2,128)S(1)} %add_rsqrt_fusion), kind=kLoop, calls=%fused_computation.10 | loop fusion | flops 1966080 | bytes 987136 | tf_op jit(solution)/shard_map/convert_element_type | solution.py:444
  3.3 0.5 reshape.57
  3.8 0.9 copy.18
  4.7 34.4 %shard_map.75 = (bf16[2,1280,96]{2,1,0:T(8,128)(2,1)}, bf16[4,1600,384]{2,1,0:T(8,128)(2,1)}) custom-call(bf16[4,2,320,96]{3,2,1,0:T(8,128)(2,1)} %bitcast.20, bf16[2,320,384]{2,1,0:T(8,128)(2,1)} %bitcast.25), custom_call_target="tpu_custom_call" | custom-call | tf_op jit(solution)/shard_map/pallas_call | solution.py:161
  39.2 0.0 copy-start.1
  39.2 1.8 %pad_slice_fusion.1 = (bf16[2,8,160,96]{3,2,1,0:T(8,128)(2,1)S(1)}, bf16[2,8,160,96]{3,2,1,0:T(8,128)(2,1)S(1)}) fusion(bf16[2,8,160,96]{3,2,1,0:T(8,128)(2,1)} %bitcast.21), kind=kLoop, calls=%fused_computation.14 | loop fusion | bytes 1474560 | tf_op jit(solution)/shard_map/slice | solution.py:453
  41.0 0.2 copy.19
  41.2 0.2 copy.21
  41.5 0.0 copy-done.1
  41.5 0.2 copy.20
  41.7 1.2 %maximum_bitcast_fusion.act_ref = bf16[2,288,1280]{2,1,0:T(8,128)(2,1)} fusion(bf16[2,1280,96]{1,2,0:T(8,128)(2,1)S(1)} %copy.21, bf16[2,1280,96]{1,2,0:T(8,128)(2,1)S(1)} %copy.20, bf16[2,1280,96]{1,2,0:T(8,128)(2,1)S(1)} %copy.19), kind=kLoop, calls=%fused_computation | loop fusion | flops 4423680 | bytes 2949120 | tf_op jit(solution)/shard_map/transpose | solution.py:454
  42.9 0.0 copy-start
  42.9 0.0 copy-start.2
  42.9 13.8 %shard_map.76.partial_ref = f32[8,9,48,288]{3,2,1,0:T(8,128)} custom-call(bf16[2,288,1280]{2,1,0:T(8,128)(2,1)} %maximum_bitcast_fusion.act_ref, bf16[4,1600,384]{2,1,0:T(8,128)(2,1)} %get-tuple-element.10.cot_ref), custom_call_target="tpu_custom_call" | custom-call | flops 5096079360 | bytes 10000000 | tf_op jit(solution)/shard_map/pallas_call | solution.py:416
  56.7 0.0 copy-done
  56.7 0.0 copy-start.4
  56.7 0.5 reshape.61
  57.2 0.9 copy.26
  58.1 0.0 copy-done.2
  58.1 0.1 convert_reduce_fusion
  58.3 0.7 reshape.63.bias_ref
  58.9 0.0 copy-done.4
  58.9 0.7 reshape.62.gain_ref
  59.6 50.0 %shard_map.77 = (f32[9,48,288]{2,1,0:T(8,128)}, bf16[4,2,320,96]{3,2,1,0:T(8,128)(2,1)}, f32[2,4,1,96]{3,2,1,0:T(1,128)}) custom-call(f32[8,9,48,288]{3,2,1,0:T(8,128)} %shard_map.76.partial_ref, bf16[4,1600,384]{2,1,0:T(8,128)(2,1)} %get-tuple-element.10.cot_ref, bf16[96,10368]{1,0:T(8,128)(2,1)} %kernel_ref.1, bf16[4,2,320,96]{3,2,1,0:T(8,128)(2,1)} %bitcast.24, ...), custom_call_target="tpu_custom_call" | custom-call | tf_op jit(solution)/shard_map/pallas_call | solution.py:360
  109.6 0.0 copy-start.3
  109.6 0.8 slice_reduce_fusion
  110.4 0.7 squeeze.6
  111.1 0.7 squeeze.7
  111.7 1.6 %reshape.65 = f32[9,48,3,96]{3,2,1,0:T(4,128)S(1)} reshape(f32[9,48,288]{2,1,0:T(8,128)} %get-tuple-element.12) | data formatting | bytes 995328 | tf_op jit(solution)/shard_map/reshape | solution.py:462
  113.4 0.9 copy.24
  114.3 0.0 copy-done.3
  114.3 0.5 copy.23
  114.8 1.2 %reshape.64 = bf16[2,2,160,384]{3,2,1,0:T(8,128)(2,1)} reshape(bf16[2,320,4,96]{3,2,1,0:T(4,128)(2,1)S(1)} %copy.23) | data formatting | bytes 983040 | tf_op jit(solution)/shard_map/reshape | solution.py:464
  (1 shorter events, 0.0 us)
Async XLA Ops:
  39.2 2.3 %copy-start.1 = (bf16[2,1280,96]{2,1,0:T(8,128)(2,1)S(1)}, bf16[2,1280,96]{2,1,0:T(8,128)(2,1)}, u32[]{:S(2)}) copy-start(bf16[2,1280,96]{2,1,0:T(8,128)(2,1)} %get-tuple-element.9) | copy-start | bytes 1474564
  42.9 13.8 %copy-start = (bf16[2,2,160,384]{3,2,1,0:T(8,128)(2,1)S(1)}, bf16[2,2,160,384]{3,2,1,0:T(8,128)(2,1)}, u32[]{:S(2)}) copy-start(bf16[2,2,160,384]{3,2,1,0:T(8,128)(2,1)} %param.4) | copy-start | bytes 1474564
  42.9 15.2 %copy-start.2 = (bf16[2,2,160,384]{3,2,1,0:T(8,128)(2,1)S(1)}, bf16[2,2,160,384]{3,2,1,0:T(8,128)(2,1)}, u32[]{:S(2)}) copy-start(bf16[2,2,160,384]{3,2,1,0:T(8,128)(2,1)} %param.7) | copy-start | bytes 1474564
  56.7 2.2 %copy-start.4 = (f32[384]{0:T(512)S(1)}, f32[384]{0:T(512)}, u32[]{:S(2)}) copy-start(f32[384]{0:T(512)} %param.5) | copy-start | bytes 4612
  109.6 4.6 %copy-start.3 = (bf16[4,2,320,96]{3,2,1,0:T(8,128)(2,1)S(1)}, bf16[4,2,320,96]{3,2,1,0:T(8,128)(2,1)}, u32[]{:S(2)}) copy-start(bf16[4,2,320,96]{3,2,1,0:T(8,128)(2,1)} %get-tuple-element.11) | copy-start | bytes 1474564

commit v4 on v3

--- a/solution.py
+++ b/solution.py
@@ -247,7 +247,7 @@
 
     span = 2 * block
 
-    def conv(f):
+    def conv(f, low, top):
         def body(step, carry):
             left = jnp.concatenate(
                 [
@@ -273,21 +273,28 @@
             )
             return carry
 
-        lax.fori_loop(0, cells // span, body, 0)
+        lax.fori_loop(low, top, body, 0)
+
+    def send_back(f):
         for d in range(1, high):
             back_copy(f, d).start()
         back[row, f] = part_of(f, row)[...]
 
-    for f in range(frames):
-        conv(f)
-        if f == 0:
-            for k in range(1, chips):
-                pair_copy(k).wait_recv()
-                mine = lax.rem(chip + k, chips) * 2 + core
-                send_buf[k - 1] = (partial_ref[mine] + pair_land[k]).astype(send_buf.dtype)
-                chip_copy(k).start()
-            pair_copy(0).wait_recv()
-            out_ref[...] = partial_ref[me] + pair_land[0]
+    conv(0, 0, 1)
+    for k in range(1, chips):
+        pair_copy(k).wait_recv()
+        mine = lax.rem(chip + k, chips) * 2 + core
+        for g in range(3):
+            sums = [partial_ref[mine, 3 * g + j] + pair_land[k, 3 * g + j] for j in range(3)]
+            send_buf[k - 1, g] = jnp.concatenate(sums, axis=-1).astype(send_buf.dtype)
+        chip_copy(k).start()
+    conv(0, 1, cells // span)
+    send_back(0)
+    for f in range(1, frames):
+        conv(f, 0, cells // span)
+        send_back(f)
+    pair_copy(0).wait_recv()
+    out_ref[...] = partial_ref[me] + pair_land[0]
     for f in range(frames):
         for d in range(1, high):
             back_copy(f, d).wait_recv()
@@ -331,7 +338,10 @@
     across[row] = middle[...]
     for k in range(1, chips):
         chip_copy(k).wait_recv()
-        out_ref[...] += recv_buf[k - 1].astype(jnp.float32)
+        for g in range(3):
+            terms = recv_buf[k - 1, g].astype(jnp.float32)
+            for j in range(3):
+                out_ref[3 * g + j] += terms[:, j * 3 * part : (j + 1) * 3 * part]
     out_ref[...] *= scale
     for d in range(1, high):
         second(d).wait_recv()
@@ -371,8 +381,8 @@
             pltpu.VMEM((frames, high * block, part), jnp.float32),
             pltpu.VMEM((high, frames, block, part), jnp.float32),
             pltpu.VMEM((chips,) + one, jnp.float32),
-            pltpu.VMEM((chips - 1,) + one, jnp.bfloat16),
-            pltpu.VMEM((chips - 1,) + one, jnp.bfloat16),
+            pltpu.VMEM((chips - 1, 3, one[1], 9 * part), jnp.bfloat16),
+            pltpu.VMEM((chips - 1, 3, one[1], 9 * part), jnp.bfloat16),
             pltpu.VMEM(stats, jnp.float32),
             pltpu.VMEM((count,) + stats, jnp.float32),
             pltpu.VMEM(stats, jnp.float32),

time: 116 us -> 108 us (0.931)
  Pallas kernels: 98.3 us -> 89.5 us
    pallas_call x1, Pallas kernels: 50 us -> 41.3 us  [finish(): pl.pallas_call(functools.partial(finish_kernel, count, high, width, scale...]
where the time goes in v4:
time: 108 us; the launch traced here: 107 us
  Pallas kernels  89.5 us (83%)
  local copies, waits for them, and re-layouts  13 us (12%)
  other arithmetic  3.98 us (4%)
    pallas_call x1, Pallas kernels, finish(): pl.pallas_call(functools.partial(finish_kernel, count, high, width, scale...  41.3 us
    pallas_call x1, Pallas kernels, exchange(): pl.pallas_call(functools.partial(exchange_kernel, count, high, width), ou...  34.4 us
    pallas_call x1, Pallas kernels, weight_grad(): pl.pallas_call(functools.partial(weight_grad_kernel, width), grid=(9,), o...  13.8 us

profile of v4, /device:TPU:0, one launch (start us, length us, event | category | flops | bytes accessed | tf_op | source)
XLA Modules:
  0.0 107.3 jit_solution(16404539903717025338)
XLA Ops:
  0.6 1.3 %fusion = f32[2,2,160]{2,1,0:T(2,128)S(1)} fusion(bf16[2,2,160,384]{3,2,1,0:T(8,128)(2,1)} %param.4), kind=kLoop, calls=%fused_computation.3 | loop fusion | flops 736640 | bytes 494080 | tf_op jit(solution)/shard_map/reduce_sum | solution.py:450
  1.9 1.4 %fusion.7 = bf16[2,2,160,384]{3,2,1,0:T(8,128)(2,1)S(1)} fusion(bf16[2,2,160,384]{3,2,1,0:T(8,128)(2,1)} %param.4, f32[384]{0:T(512)} %param.5, f32[2,2,160]{2,1,0:T(2,128)S(1)} %add_rsqrt_fusion), kind=kLoop, calls=%fused_computation.10 | loop fusion | flops 1966080 | bytes 987136 | tf_op jit(solution)/shard_map/convert_element_type | solution.py:454
  3.3 0.5 reshape.57
  3.8 0.9 copy.18
  4.7 34.4 %shard_map.75 = (bf16[2,1280,96]{2,1,0:T(8,128)(2,1)}, bf16[4,1600,384]{2,1,0:T(8,128)(2,1)}) custom-call(bf16[4,2,320,96]{3,2,1,0:T(8,128)(2,1)} %bitcast.20, bf16[2,320,384]{2,1,0:T(8,128)(2,1)} %bitcast.25), custom_call_target="tpu_custom_call" | custom-call | tf_op jit(solution)/shard_map/pallas_call | solution.py:161
  39.2 0.0 copy-start.1
  39.2 1.8 %pad_slice_fusion.1 = (bf16[2,8,160,96]{3,2,1,0:T(8,128)(2,1)S(1)}, bf16[2,8,160,96]{3,2,1,0:T(8,128)(2,1)S(1)}) fusion(bf16[2,8,160,96]{3,2,1,0:T(8,128)(2,1)} %bitcast.21), kind=kLoop, calls=%fused_computation.14 | loop fusion | bytes 1474560 | tf_op jit(solution)/shard_map/slice | solution.py:463
  41.0 0.2 copy.19
  41.2 0.2 copy.21
  41.5 0.0 copy-done.1
  41.5 0.2 copy.20
  41.7 1.2 %maximum_bitcast_fusion.act_ref = bf16[2,288,1280]{2,1,0:T(8,128)(2,1)} fusion(bf16[2,1280,96]{1,2,0:T(8,128)(2,1)S(1)} %copy.21, bf16[2,1280,96]{1,2,0:T(8,128)(2,1)S(1)} %copy.20, bf16[2,1280,96]{1,2,0:T(8,128)(2,1)S(1)} %copy.19), kind=kLoop, calls=%fused_computation | loop fusion | flops 4423680 | bytes 2949120 | tf_op jit(solution)/shard_map/transpose | solution.py:464
  42.9 0.0 copy-start
  42.9 0.0 copy-start.2
  42.9 13.8 %shard_map.76.partial_ref = f32[8,9,48,288]{3,2,1,0:T(8,128)} custom-call(bf16[2,288,1280]{2,1,0:T(8,128)(2,1)} %maximum_bitcast_fusion.act_ref, bf16[4,1600,384]{2,1,0:T(8,128)(2,1)} %get-tuple-element.10.cot_ref), custom_call_target="tpu_custom_call" | custom-call | flops 5096079360 | bytes 10000000 | tf_op jit(solution)/shard_map/pallas_call | solution.py:426
  56.7 0.0 copy-done
  56.7 0.0 copy-start.4
  56.7 0.5 reshape.61
  57.2 0.9 copy.26
  58.1 0.0 copy-done.2
  58.1 0.1 convert_reduce_fusion
  58.3 0.7 reshape.63.bias_ref
  58.9 0.0 copy-done.4
  58.9 0.7 reshape.62.gain_ref
  59.6 41.3 %shard_map.77 = (f32[9,48,288]{2,1,0:T(8,128)}, bf16[4,2,320,96]{3,2,1,0:T(8,128)(2,1)}, f32[2,4,1,96]{3,2,1,0:T(1,128)}) custom-call(f32[8,9,48,288]{3,2,1,0:T(8,128)} %shard_map.76.partial_ref, bf16[4,1600,384]{2,1,0:T(8,128)(2,1)} %get-tuple-element.10.cot_ref, bf16[96,10368]{1,0:T(8,128)(2,1)} %kernel_ref.1, bf16[4,2,320,96]{3,2,1,0:T(8,128)(2,1)} %bitcast.24, ...), custom_call_target="tpu_custom_call" | custom-call | tf_op jit(solution)/shard_map/pallas_call | solution.py:370
  100.9 0.0 copy-start.3
  100.9 0.8 slice_reduce_fusion
  101.7 0.7 squeeze.6
  102.4 0.7 squeeze.7
  103.0 1.6 %reshape.65 = f32[9,48,3,96]{3,2,1,0:T(4,128)S(1)} reshape(f32[9,48,288]{2,1,0:T(8,128)} %get-tuple-element.12) | data formatting | bytes 995328 | tf_op jit(solution)/shard_map/reshape | solution.py:472
  104.7 0.9 copy.24
  105.6 0.0 copy-done.3
  105.6 0.5 copy.23
  106.1 1.2 %reshape.64 = bf16[2,2,160,384]{3,2,1,0:T(8,128)(2,1)} reshape(bf16[2,320,4,96]{3,2,1,0:T(4,128)(2,1)S(1)} %copy.23) | data formatting | bytes 983040 | tf_op jit(solution)/shard_map/reshape | solution.py:474
  (1 shorter events, 0.0 us)
Async XLA Ops:
  39.2 2.3 %copy-start.1 = (bf16[2,1280,96]{2,1,0:T(8,128)(2,1)S(1)}, bf16[2,1280,96]{2,1,0:T(8,128)(2,1)}, u32[]{:S(2)}) copy-start(bf16[2,1280,96]{2,1,0:T(8,128)(2,1)} %get-tuple-element.9) | copy-start | bytes 1474564
  42.9 13.8 %copy-start = (bf16[2,2,160,384]{3,2,1,0:T(8,128)(2,1)S(1)}, bf16[2,2,160,384]{3,2,1,0:T(8,128)(2,1)}, u32[]{:S(2)}) copy-start(bf16[2,2,160,384]{3,2,1,0:T(8,128)(2,1)} %param.4) | copy-start | bytes 1474564
  42.9 15.2 %copy-start.2 = (bf16[2,2,160,384]{3,2,1,0:T(8,128)(2,1)S(1)}, bf16[2,2,160,384]{3,2,1,0:T(8,128)(2,1)}, u32[]{:S(2)}) copy-start(bf16[2,2,160,384]{3,2,1,0:T(8,128)(2,1)} %param.7) | copy-start | bytes 1474564
  56.7 2.2 %copy-start.4 = (f32[384]{0:T(512)S(1)}, f32[384]{0:T(512)}, u32[]{:S(2)}) copy-start(f32[384]{0:T(512)} %param.5) | copy-start | bytes 4612
  100.9 4.6 %copy-start.3 = (bf16[4,2,320,96]{3,2,1,0:T(8,128)(2,1)S(1)}, bf16[4,2,320,96]{3,2,1,0:T(8,128)(2,1)}, u32[]{:S(2)}) copy-start(bf16[4,2,320,96]{3,2,1,0:T(8,128)(2,1)} %get-tuple-element.11) | copy-start | bytes 1474564
